TPU v7x, 256 devices: a whole 4x4x8 slice. The times are simulated.
256 devices in a mesh: gx: 8 (over x, core), gy: 4 (over y), al: 8 (over z).
Axes of the slice: x: 4, y: 4, z: 8, core: 2. Of those that a mesh axis runs over, the one named last changes fastest.
Arguments:
- volt_now: float32 [16, 512, 2048], P('al', 'gx', 'gy'), may hold values from -8 to 8
- volt_prev: float32 [16, 512, 2048], P('al', 'gx', 'gy'), may hold values from -8 to 8
- cap_term: float32 [16, 512, 2048], P('al', 'gx', 'gy'), may hold values from 0.05 to 0.5
- edge_x: float32 [16, 512, 2048], P('al', 'gx', 'gy'), may hold values from 0.2 to 5
- edge_y: float32 [16, 512, 2048], P('al', 'gx', 'gy'), may hold values from 0.2 to 5
- via_below: float32 [16, 512, 2048], P('al', 'gx', 'gy'), may hold values from 0.5 to 8
- cell_ids: int32 [512, 2048], P('gx', 'gy'), may hold values from 0 to 63
- placed: int32 [512, 2048], P('gx', 'gy'), may hold values 0 or 1
- current_table: float32 [64], replicated, may hold values from 0.5 to 4
Outputs:
- solution_field: float32 [16, 512, 2048], P('al', 'gx', 'gy')
- residual: float32 [16, 512, 2048], P('al', 'gx', 'gy')
All inputs are finite; a program needn't handle non-finite values. No bound on the sum of `placed` on one device may be relied on, other than what follows from the above.
Results may differ from a plain program's by a relative error of at most 0.0059.
Values sent between devices are 32-bit elements; how exact they have to be, the bound alone decides.
A program may use at most 64 MiB of HBM per device.

v0:
```python
import jax
import jax.numpy as jnp
from jax import lax
from jax.sharding import PartitionSpec as P

ITERS = 8


def extended(cells, sides, width):
    for axis, dim in sides:
        count = lax.axis_size(axis)
        ends = count - 1
        head = lax.slice_in_dim(cells, 0, width, axis=dim)
        tail = lax.slice_in_dim(cells, cells.shape[dim] - width, cells.shape[dim], axis=dim)
        cells = jnp.concatenate(
            [
                lax.ppermute(tail, axis, [(i, (i + 1) % count) for i in range(ends)]),
                cells,
                lax.ppermute(head, axis, [((i + 1) % count, i) for i in range(ends)]),
            ],
            axis=dim,
        )
    return cells


def carried_in(part, axis, combine, identity, reverse):
    count = lax.axis_size(axis)
    place = lax.axis_index(axis)
    ahead = count - 1 - place if reverse else place
    gathered = jax.tree.map(lambda a: lax.all_gather(a, axis), part)
    state = jax.tree.map(lambda a, e: jnp.zeros_like(a) + jnp.asarray(e, a.dtype), part, identity)

    def one(lap, state):
        source = count - 1 - lap if reverse else lap
        return combine(
            state, jax.tree.map(lambda a: lax.dynamic_index_in_dim(a, source, 0, False), gathered)
        )

    return lax.fori_loop(0, ahead, one, state)


def matrix_norm(mat):
    scale = jnp.maximum(
        jnp.maximum(jnp.abs(mat[0]), jnp.abs(mat[1])), jnp.maximum(jnp.abs(mat[2]), jnp.abs(mat[3]))
    )
    return (mat[0] / scale, mat[1] / scale, mat[2] / scale, mat[3] / scale)


def matrix_join(earlier, later):
    top_left = later[0] * earlier[0] + later[1] * earlier[2]
    top_right = later[0] * earlier[1] + later[1] * earlier[3]
    low_left = later[2] * earlier[0] + later[3] * earlier[2]
    low_right = later[2] * earlier[1] + later[3] * earlier[3]
    return matrix_norm((top_left, top_right, low_left, low_right))


def affine_join(earlier, later):
    return (earlier[0] * later[0], later[0] * earlier[1] + later[1])


def inner_sum(resid, zvec):
    return lax.psum(jnp.sum(resid * zvec), ("gx", "gy", "al"))


def run_solver(rhs, precond, operate):
    solution_field = jnp.zeros_like(rhs)
    residual = rhs
    zvec = precond(residual)
    rho = inner_sum(residual, zvec)
    direction = zvec
    for step in range(ITERS):
        image = operate(direction)
        alpha = rho / lax.psum(jnp.sum(direction * image), ("gx", "gy", "al"))
        solution_field = solution_field + alpha * direction
        residual = residual - alpha * image
        if step + 1 < ITERS:
            zvec = precond(residual)
            rho_new = inner_sum(residual, zvec)
            direction = zvec + rho_new / rho * direction
            rho = rho_new
    return (solution_field, residual)


def shards(
    volt_now, volt_prev, cap_term, edge_x, edge_y, via_below, cell_ids, placed, current_table
):
    types = lax.broadcasted_iota(jnp.int32, (current_table.shape[0],) + cell_ids.shape, 0)
    chosen = jnp.sum(jnp.where(cell_ids[None] == types, current_table[:, None, None], 0.0), axis=0)
    current = chosen * placed.astype(jnp.float32)
    layers, cols, rows = volt_now.shape
    shape = volt_now.shape
    li = lax.broadcasted_iota(jnp.int32, shape, 0) + lax.axis_index("al") * layers
    xi = lax.broadcasted_iota(jnp.int32, shape, 1) + lax.axis_index("gx") * cols
    yi = lax.broadcasted_iota(jnp.int32, shape, 2) + lax.axis_index("gy") * rows
    ex = jnp.where(xi < cols * lax.axis_size("gx") - 1, edge_x, 0.0)
    ey = jnp.where(yi < rows * lax.axis_size("gy") - 1, edge_y, 0.0)
    vb = jnp.where(li > 0, via_below, 0.0)
    rims = extended(jnp.stack([ex, ey, vb]), (("gx", 2), ("gy", 3), ("al", 1)), 1)
    exl = rims[0, 1:-1, :-2, 1:-1]
    eyl = rims[1, 1:-1, 1:-1, :-2]
    via_below_admittance = rims[2, 2:, 1:-1, 1:-1]
    diag = cap_term + ex + exl + ey + eyl + vb + via_below_admittance
    stamp = jnp.where(li == 0, current[None], 0.0)
    rhs = cap_term * (4.0 * volt_now - volt_prev) / 3.0 + stamp
    unit = jnp.ones((cols, rows), jnp.float32)
    naught = jnp.zeros((cols, rows), jnp.float32)
    local_mat = (unit, naught, naught, unit)
    for layer_position in range(layers):
        g_sq = vb[layer_position] * vb[layer_position]
        local_mat = matrix_norm(
            (
                diag[layer_position] * local_mat[0] - g_sq * local_mat[2],
                diag[layer_position] * local_mat[1] - g_sq * local_mat[3],
                local_mat[0],
                local_mat[1],
            )
        )
    below = carried_in(local_mat, "al", matrix_join, (unit, naught, naught, unit), False)
    prior = (below[0] + below[1]) / (below[2] + below[3])
    pivot_rows = []
    for layer_position in range(layers):
        prior = diag[layer_position] - vb[layer_position] * vb[layer_position] / prior
        pivot_rows.append(prior)
    work_vector = jnp.stack(pivot_rows)
    up_coef = vb / work_vector
    downward_coefficient = via_below_admittance / work_vector

    def precond(r):
        scaled = r / work_vector
        factor_mappings = (unit, naught)
        for layer_position in range(layers):
            factor_mappings = (
                factor_mappings[0] * up_coef[layer_position],
                up_coef[layer_position] * factor_mappings[1] + scaled[layer_position],
            )
        inbound_value = carried_in(factor_mappings, "al", affine_join, (unit, naught), False)[1]
        eliminated_factor = []
        for layer_position in range(layers):
            inbound_value = up_coef[layer_position] * inbound_value + scaled[layer_position]
            eliminated_factor.append(inbound_value)
        factor_mappings = (unit, naught)
        for layer_position in range(layers - 1, -1, -1):
            factor_mappings = (
                downward_coefficient[layer_position] * factor_mappings[0],
                downward_coefficient[layer_position] * factor_mappings[1]
                + eliminated_factor[layer_position],
            )
        layer_overhead = carried_in(factor_mappings, "al", affine_join, (unit, naught), True)[1]
        result = [None] * layers
        for layer_position in range(layers - 1, -1, -1):
            layer_overhead = (
                eliminated_factor[layer_position]
                + downward_coefficient[layer_position] * layer_overhead
            )
            result[layer_position] = layer_overhead
        return jnp.stack(result)

    def operate(v):
        padded = extended(v, (("gx", 1), ("gy", 2), ("al", 0)), 1)
        side = ex * padded[1:-1, 2:, 1:-1] + exl * padded[1:-1, :-2, 1:-1]
        side = side + ey * padded[1:-1, 1:-1, 2:] + eyl * padded[1:-1, 1:-1, :-2]
        side = side + via_below_admittance * padded[2:, 1:-1, 1:-1] + vb * padded[:-2, 1:-1, 1:-1]
        return diag * v - side

    return run_solver(rhs, precond, operate)


def solution(mesh):
    placed = (
        P("al", "gx", "gy"),
        P("al", "gx", "gy"),
        P("al", "gx", "gy"),
        P("al", "gx", "gy"),
        P("al", "gx", "gy"),
        P("al", "gx", "gy"),
        P("gx", "gy"),
        P("gx", "gy"),
        P(),
    )
    return jax.shard_map(
        shards,
        mesh=mesh,
        in_specs=placed,
        out_specs=(P("al", "gx", "gy"), P("al", "gx", "gy")),
        check_vma=False,
    )
```

profile of v0, /device:TPU:1, one launch (start us, length us, event | category | flops | bytes accessed | tf_op | source)
XLA Modules:
  0.0 2461.7 jit_solution(4861785161455513537)
XLA Ops:
  52.4 33.8 %all-gather.31.cloned.1.call-done = f32[8,64,512]{2,1,0:T(8,128)} async-done(((f32[1,64,512]{2,1,0:T(8,128)}), f32[8,64,512]{2,1,0:T(8,128)}) %all-gather.31.cloned.1.call-update) | async-done | bytes 1048592 | tf_op jit(solution)/shard_map/all_gather | solution.py:30
  86.2 39.6 %all-gather.33.cloned.1.call-done = f32[8,64,512]{2,1,0:T(8,128)} async-done(((f32[1,64,512]{2,1,0:T(8,128)}), f32[8,64,512]{2,1,0:T(8,128)}) %all-gather.33.cloned.1.call-update) | async-done | bytes 1048592 | tf_op jit(solution)/shard_map/all_gather | solution.py:30
  125.8 39.0 %all-gather.35.cloned.1.call-done = f32[8,64,512]{2,1,0:T(8,128)} async-done(((f32[1,64,512]{2,1,0:T(8,128)}), f32[8,64,512]{2,1,0:T(8,128)}) %all-gather.35.cloned.1.call-update) | async-done | bytes 1048592 | tf_op jit(solution)/shard_map/all_gather | solution.py:30
  164.8 39.5 %all-gather.37.cloned.1.call-done = f32[8,64,512]{2,1,0:T(8,128)} async-done(((f32[1,64,512]{2,1,0:T(8,128)}), f32[8,64,512]{2,1,0:T(8,128)}) %all-gather.37.cloned.1.call-update) | async-done | bytes 1048592 | tf_op jit(solution)/shard_map/all_gather | solution.py:30
  208.0 43.8 %all-gather.39.cloned.1.call-done = f32[8,64,512]{2,1,0:T(8,128)} async-done(((f32[1,64,512]{2,1,0:T(8,128)}), f32[8,64,512]{2,1,0:T(8,128)}) %all-gather.39.cloned.1.call-update) | async-done | bytes 1048592 | tf_op jit(solution)/shard_map/all_gather | solution.py:30
  251.9 39.5 %all-gather.41.cloned.1.call-done = f32[8,64,512]{2,1,0:T(8,128)} async-done(((f32[1,64,512]{2,1,0:T(8,128)}), f32[8,64,512]{2,1,0:T(8,128)}) %all-gather.41.cloned.1.call-update) | async-done | bytes 1048592 | tf_op jit(solution)/shard_map/all_gather | solution.py:30
  292.2 38.2 %all-gather.43.cloned.1.call-done = f32[8,64,512]{2,1,0:T(8,128)} async-done(((f32[1,64,512]{2,1,0:T(8,128)}), f32[8,64,512]{2,1,0:T(8,128)}) %all-gather.43.cloned.1.call-update) | async-done | bytes 1048592 | tf_op jit(solution)/shard_map/all_gather | solution.py:30
  330.4 39.6 %all-gather.59.cloned.1.call-done = f32[512,512]{1,0:T(8,128)} async-done(((f32[64,512]{1,0:T(8,128)}), f32[512,512]{1,0:T(8,128)}) %all-gather.59.cloned.1.call-update) | async-done | bytes 1048592 | tf_op jit(solution)/shard_map/all_gather | solution.py:30
  406.8 76.7 %all-reduce = (f32[]{:T(128)}, f32[]{:T(128)}) all-reduce(f32[]{:T(128)} %get-tuple-element.1105, f32[]{:T(128)} %get-tuple-element.1104), channel_id=1, replica_groups=mesh['gx'=8,'gy'=4,'al'=8] {'gx','gy','al'}, use_global_device_ids=true, to_apply=%region_8.9 | all-reduce | flops 2 | bytes 16 | tf_op jit(solution)/shard_map/psum | solution.py:62
  488.3 29.0 %all-gather.45.cloned.1.call-done = f32[8,64,512]{2,1,0:T(8,128)} async-done(((f32[1,64,512]{2,1,0:T(8,128)}), f32[8,64,512]{2,1,0:T(8,128)}) %all-gather.45.cloned.1.call-update) | async-done | bytes 1048592 | tf_op jit(solution)/shard_map/all_gather | solution.py:30
  520.0 47.6 %all-gather.61.cloned.1.call-done = f32[512,512]{1,0:T(8,128)} async-done(((f32[64,512]{1,0:T(8,128)}), f32[512,512]{1,0:T(8,128)}) %all-gather.61.cloned.1.call-update) | async-done | bytes 1048592 | tf_op jit(solution)/shard_map/all_gather | solution.py:30
  582.2 78.9 %psum.114 = f32[]{:T(128)} all-reduce(f32[]{:T(128)} %multiply_reduce_fusion.13), channel_id=1, replica_groups=mesh['gx'=8,'gy'=4,'al'=8] {'gx','gy','al'}, use_global_device_ids=true, to_apply=%region_16.17 | all-reduce | flops 1 | bytes 8 | tf_op jit(solution)/shard_map/psum | solution.py:62
  690.2 75.0 %psum.115 = f32[]{:T(128)} all-reduce(f32[]{:T(128)} %get-tuple-element.1341), channel_id=1, replica_groups=mesh['gx'=8,'gy'=4,'al'=8] {'gx','gy','al'}, use_global_device_ids=true, to_apply=%region_18.19 | all-reduce | flops 1 | bytes 8 | tf_op jit(solution)/shard_map/psum | solution.py:73
  801.3 47.5 %all-gather.63.cloned.1.call-done = f32[512,512]{1,0:T(8,128)} async-done(((f32[64,512]{1,0:T(8,128)}), f32[512,512]{1,0:T(8,128)}) %all-gather.63.cloned.1.call-update) | async-done | bytes 1048592 | tf_op jit(solution)/shard_map/all_gather | solution.py:30
  863.6 79.1 %psum.116 = f32[]{:T(128)} all-reduce(f32[]{:T(128)} %multiply_reduce_fusion.11), channel_id=1, replica_groups=mesh['gx'=8,'gy'=4,'al'=8] {'gx','gy','al'}, use_global_device_ids=true, to_apply=%region_24.25 | all-reduce | flops 1 | bytes 8 | tf_op jit(solution)/shard_map/psum | solution.py:62
  972.0 75.0 %psum.117 = f32[]{:T(128)} all-reduce(f32[]{:T(128)} %get-tuple-element.1333), channel_id=1, replica_groups=mesh['gx'=8,'gy'=4,'al'=8] {'gx','gy','al'}, use_global_device_ids=true, to_apply=%region_26.27 | all-reduce | flops 1 | bytes 8 | tf_op jit(solution)/shard_map/psum | solution.py:73
  1051.8 28.8 %all-gather.49.cloned.1.call-done = f32[8,64,512]{2,1,0:T(8,128)} async-done(((f32[1,64,512]{2,1,0:T(8,128)}), f32[8,64,512]{2,1,0:T(8,128)}) %all-gather.49.cloned.1.call-update) | async-done | bytes 1048592 | tf_op jit(solution)/shard_map/all_gather | solution.py:30
  1083.1 47.6 %all-gather.65.cloned.1.call-done = f32[512,512]{1,0:T(8,128)} async-done(((f32[64,512]{1,0:T(8,128)}), f32[512,512]{1,0:T(8,128)}) %all-gather.65.cloned.1.call-update) | async-done | bytes 1048592 | tf_op jit(solution)/shard_map/all_gather | solution.py:30
  1145.3 78.9 %psum.118 = f32[]{:T(128)} all-reduce(f32[]{:T(128)} %multiply_reduce_fusion.9), channel_id=1, replica_groups=mesh['gx'=8,'gy'=4,'al'=8] {'gx','gy','al'}, use_global_device_ids=true, to_apply=%region_32.33 | all-reduce | flops 1 | bytes 8 | tf_op jit(solution)/shard_map/psum | solution.py:62
  1253.6 75.0 %psum.119 = f32[]{:T(128)} all-reduce(f32[]{:T(128)} %get-tuple-element.1325), channel_id=1, replica_groups=mesh['gx'=8,'gy'=4,'al'=8] {'gx','gy','al'}, use_global_device_ids=true, to_apply=%region_34.35 | all-reduce | flops 1 | bytes 8 | tf_op jit(solution)/shard_map/psum | solution.py:73
  1364.7 47.6 %all-gather.67.cloned.1.call-done = f32[512,512]{1,0:T(8,128)} async-done(((f32[64,512]{1,0:T(8,128)}), f32[512,512]{1,0:T(8,128)}) %all-gather.67.cloned.1.call-update) | async-done | bytes 1048592 | tf_op jit(solution)/shard_map/all_gather | solution.py:30
  1427.0 78.9 %psum.120 = f32[]{:T(128)} all-reduce(f32[]{:T(128)} %multiply_reduce_fusion.7), channel_id=1, replica_groups=mesh['gx'=8,'gy'=4,'al'=8] {'gx','gy','al'}, use_global_device_ids=true, to_apply=%region_40.41 | all-reduce | flops 1 | bytes 8 | tf_op jit(solution)/shard_map/psum | solution.py:62
  1535.4 75.0 %psum.121 = f32[]{:T(128)} all-reduce(f32[]{:T(128)} %get-tuple-element.1317), channel_id=1, replica_groups=mesh['gx'=8,'gy'=4,'al'=8] {'gx','gy','al'}, use_global_device_ids=true, to_apply=%region_42.43 | all-reduce | flops 1 | bytes 8 | tf_op jit(solution)/shard_map/psum | solution.py:73
  1646.5 47.6 %all-gather.69.cloned.1.call-done = f32[512,512]{1,0:T(8,128)} async-done(((f32[64,512]{1,0:T(8,128)}), f32[512,512]{1,0:T(8,128)}) %all-gather.69.cloned.1.call-update) | async-done | bytes 1048592 | tf_op jit(solution)/shard_map/all_gather | solution.py:30
  1708.7 78.9 %psum.122 = f32[]{:T(128)} all-reduce(f32[]{:T(128)} %multiply_reduce_fusion.5), channel_id=1, replica_groups=mesh['gx'=8,'gy'=4,'al'=8] {'gx','gy','al'}, use_global_device_ids=true, to_apply=%region_48.49 | all-reduce | flops 1 | bytes 8 | tf_op jit(solution)/shard_map/psum | solution.py:62
  1817.5 75.0 %psum.123 = f32[]{:T(128)} all-reduce(f32[]{:T(128)} %get-tuple-element.1309), channel_id=1, replica_groups=mesh['gx'=8,'gy'=4,'al'=8] {'gx','gy','al'}, use_global_device_ids=true, to_apply=%region_50.51 | all-reduce | flops 1 | bytes 8 | tf_op jit(solution)/shard_map/psum | solution.py:73
  1928.6 47.5 %all-gather.71.cloned.1.call-done = f32[512,512]{1,0:T(8,128)} async-done(((f32[64,512]{1,0:T(8,128)}), f32[512,512]{1,0:T(8,128)}) %all-gather.71.cloned.1.call-update) | async-done | bytes 1048592 | tf_op jit(solution)/shard_map/all_gather | solution.py:30
  1990.8 78.9 %psum.124 = f32[]{:T(128)} all-reduce(f32[]{:T(128)} %multiply_reduce_fusion.3), channel_id=1, replica_groups=mesh['gx'=8,'gy'=4,'al'=8] {'gx','gy','al'}, use_global_device_ids=true, to_apply=%region_56.57 | all-reduce | flops 1 | bytes 8 | tf_op jit(solution)/shard_map/psum | solution.py:62
  2099.5 75.0 %psum.125 = f32[]{:T(128)} all-reduce(f32[]{:T(128)} %get-tuple-element.1301), channel_id=1, replica_groups=mesh['gx'=8,'gy'=4,'al'=8] {'gx','gy','al'}, use_global_device_ids=true, to_apply=%region_58.59 | all-reduce | flops 1 | bytes 8 | tf_op jit(solution)/shard_map/psum | solution.py:73
  2210.4 47.5 %all-gather.73.cloned.1.call-done = f32[512,512]{1,0:T(8,128)} async-done(((f32[64,512]{1,0:T(8,128)}), f32[512,512]{1,0:T(8,128)}) %all-gather.73.cloned.1.call-update) | async-done | bytes 1048592 | tf_op jit(solution)/shard_map/all_gather | solution.py:30
  2268.6 78.9 %psum.126 = f32[]{:T(128)} all-reduce(f32[]{:T(128)} %multiply_reduce_fusion.1), channel_id=1, replica_groups=mesh['gx'=8,'gy'=4,'al'=8] {'gx','gy','al'}, use_global_device_ids=true, to_apply=%region_64.65 | all-reduce | flops 1 | bytes 8 | tf_op jit(solution)/shard_map/psum | solution.py:62
  2376.8 75.0 %psum.127 = f32[]{:T(128)} all-reduce(f32[]{:T(128)} %get-tuple-element.1293), channel_id=1, replica_groups=mesh['gx'=8,'gy'=4,'al'=8] {'gx','gy','al'}, use_global_device_ids=true, to_apply=%region_66.67 | all-reduce | flops 1 | bytes 8 | tf_op jit(solution)/shard_map/psum | solution.py:73
  (539 shorter events, 650.7 us)
Async XLA Ops:
  7.2 79.1 %all-gather.31.cloned.1.call-start = ((), (), s32[]{:S(2)}) async-start(), calls=%async_computation | async-start | bytes 1179648 | tf_op jit(solution)/shard_map/all_gather | solution.py:30
  22.4 8.0 collective-permute-start.3
  31.2 15.3 collective-permute-start.4
  48.6 77.2 %all-gather.33.cloned.1.call-start = ((), (), s32[]{:S(2)}) async-start(), calls=%async_computation.1 | async-start | bytes 1179648 | tf_op jit(solution)/shard_map/all_gather | solution.py:30
  49.4 115.5 %all-gather.35.cloned.1.call-start = ((), (), s32[]{:S(2)}) async-start(), calls=%async_computation.2 | async-start | bytes 1179648 | tf_op jit(solution)/shard_map/all_gather | solution.py:30
  50.1 154.2 %all-gather.37.cloned.1.call-start = ((), (), s32[]{:S(2)}) async-start(), calls=%async_computation.3 | async-start | bytes 1179648 | tf_op jit(solution)/shard_map/all_gather | solution.py:30
  50.7 201.2 %all-gather.39.cloned.1.call-start = ((), (), s32[]{:S(2)}) async-start(), calls=%async_computation.4 | async-start | bytes 1179648 | tf_op jit(solution)/shard_map/all_gather | solution.py:30
  206.7 84.7 %all-gather.41.cloned.1.call-start = ((), (), s32[]{:S(2)}) async-start(), calls=%async_computation.5 | async-start | bytes 1179648 | tf_op jit(solution)/shard_map/all_gather | solution.py:30
  207.2 123.1 %all-gather.43.cloned.1.call-start = ((), (), s32[]{:S(2)}) async-start(), calls=%async_computation.6 | async-start | bytes 1179648 | tf_op jit(solution)/shard_map/all_gather | solution.py:30
  208.0 162.0 %all-gather.59.cloned.1.call-start = ((), (), s32[]{:S(2)}) async-start(), calls=%async_computation.14 | async-start | bytes 1179648 | tf_op jit(solution)/shard_map/all_gather | solution.py:30
  292.1 225.2 %all-gather.45.cloned.1.call-start = ((), (), s32[]{:S(2)}) async-start(), calls=%async_computation.7 | async-start | bytes 1179648 | tf_op jit(solution)/shard_map/all_gather | solution.py:30
  377.5 10.7 collective-permute-start.5
  397.8 7.1 collective-permute-start.9
  488.2 79.3 %all-gather.61.cloned.1.call-start = ((), (), s32[]{:S(2)}) async-start(), calls=%async_computation.15 | async-start | bytes 1179648 | tf_op jit(solution)/shard_map/all_gather | solution.py:30
  519.9 278.8 %all-gather.47.cloned.1.call-start = ((), (), s32[]{:S(2)}) async-start(), calls=%async_computation.8 | async-start | bytes 1179648 | tf_op jit(solution)/shard_map/all_gather | solution.py:30
  681.2 7.1 collective-permute-start.15
  769.9 78.9 %all-gather.63.cloned.1.call-start = ((), (), s32[]{:S(2)}) async-start(), calls=%async_computation.16 | async-start | bytes 1179648 | tf_op jit(solution)/shard_map/all_gather | solution.py:30
  801.2 279.3 %all-gather.49.cloned.1.call-start = ((), (), s32[]{:S(2)}) async-start(), calls=%async_computation.9 | async-start | bytes 1179648 | tf_op jit(solution)/shard_map/all_gather | solution.py:30
  963.0 7.1 collective-permute-start.21
  1051.7 78.9 %all-gather.65.cloned.1.call-start = ((), (), s32[]{:S(2)}) async-start(), calls=%async_computation.17 | async-start | bytes 1179648 | tf_op jit(solution)/shard_map/all_gather | solution.py:30
  1083.1 279.1 %all-gather.51.cloned.1.call-start = ((), (), s32[]{:S(2)}) async-start(), calls=%async_computation.10 | async-start | bytes 1179648 | tf_op jit(solution)/shard_map/all_gather | solution.py:30
  1244.6 7.1 collective-permute-start.27
  1333.3 78.9 %all-gather.67.cloned.1.call-start = ((), (), s32[]{:S(2)}) async-start(), calls=%async_computation.18 | async-start | bytes 1179648 | tf_op jit(solution)/shard_map/all_gather | solution.py:30
  1364.6 279.3 %all-gather.53.cloned.1.call-start = ((), (), s32[]{:S(2)}) async-start(), calls=%async_computation.11 | async-start | bytes 1179648 | tf_op jit(solution)/shard_map/all_gather | solution.py:30
  1526.4 7.1 collective-permute-start.33
  1615.1 78.9 %all-gather.69.cloned.1.call-start = ((), (), s32[]{:S(2)}) async-start(), calls=%async_computation.19 | async-start | bytes 1179648 | tf_op jit(solution)/shard_map/all_gather | solution.py:30
  1646.4 279.6 %all-gather.55.cloned.1.call-start = ((), (), s32[]{:S(2)}) async-start(), calls=%async_computation.12 | async-start | bytes 1179648 | tf_op jit(solution)/shard_map/all_gather | solution.py:30
  1808.5 7.1 collective-permute-start.39
  1897.2 78.8 %all-gather.71.cloned.1.call-start = ((), (), s32[]{:S(2)}) async-start(), calls=%async_computation.20 | async-start | bytes 1179648 | tf_op jit(solution)/shard_map/all_gather | solution.py:30
  1928.5 279.4 %all-gather.57.cloned.1.call-start = ((), (), s32[]{:S(2)}) async-start(), calls=%async_computation.13 | async-start | bytes 1179648 | tf_op jit(solution)/shard_map/all_gather | solution.py:30
  2179.2 78.8 %all-gather.73.cloned.1.call-start = ((), (), s32[]{:S(2)}) async-start(), calls=%async_computation.21 | async-start | bytes 1179648 | tf_op jit(solution)/shard_map/all_gather | solution.py:30
  2367.7 7.3 collective-permute-start.51
  (135 other events, 3697.4 us)
Sparse Core Ops, SparseCore 0:
  48.7 37.4 all-gather.30
  88.6 37.1 all-gather.32
  127.6 37.1 all-gather.34
  167.1 37.1 all-gather.36
  206.8 45.0 all-gather.38
  254.1 37.1 all-gather.40
  293.1 37.1 all-gather.42
  332.7 37.1 all-gather.58
  488.3 28.9 all-gather.44
  520.0 47.4 all-gather.60
  770.1 28.6 all-gather.46
  801.4 47.4 all-gather.62
  1051.9 28.6 all-gather.48
  1083.2 47.4 all-gather.64
  1333.5 28.6 all-gather.50
  1364.7 47.4 all-gather.66
  1615.2 28.6 all-gather.52
  1646.5 47.4 all-gather.68
  1897.4 28.6 all-gather.54
  1928.7 47.3 all-gather.70
  2179.3 28.6 all-gather.56
  2210.6 47.3 all-gather.72
where the time goes:
time: 2470 us; the launch traced here: 2460 us
  blocking collectives  1150 us (47%)
  waiting for transfers between devices  940 us (38%)
  other arithmetic  166 us (7%)
  starting transfers between devices  144 us (6%)
  between operations  36.1 us (1%)
    all_gather x22, waiting for transfers between devices, carried_in(): gathered = jax.tree.map(lambda a: lax.all_gather(a, axis), part)  847 us
    psum x8, blocking collectives, inner_sum(): return lax.psum(jnp.sum(resid * zvec), ('gx', 'gy', 'al'))  629 us
    psum x7, blocking collectives, run_solver(): alpha = rho / lax.psum(jnp.sum(direction * image), ('gx', 'gy', 'al'))  525 us
    ppermute x26, starting transfers between devices, extended(): lax.ppermute(tail, axis, [(i, (i + 1) % count) for i in range(ends)])  90.9 us
    add x56, other arithmetic, affine_join(): return (earlier[0] * later[0], later[0] * earlier[1] + later[1])  83.2 us
    ppermute x27, waiting for transfers between devices, extended(): lax.ppermute(head, axis, [((i + 1) % count, i) for i in range(ends)])  57.9 us
    ppermute x27, starting transfers between devices, extended(): lax.ppermute(head, axis, [((i + 1) % count, i) for i in range(ends)])  52.4 us
  transfers between devices with their start and end apart: 75, of which 66 were waited for; matrix products, arithmetic and copies ran while one was open for 0% of the time, Pallas kernels for 0%

commit v1 on v0

v1 whole, which is shorter than its diff:
```python
import functools

import jax
import jax.numpy as jnp
from jax import lax
from jax.experimental import pallas as pl
from jax.experimental.pallas import tpu as pltpu
from jax.sharding import PartitionSpec as P

ITERS = 8
MESH = pl.DeviceIdType.MESH
EX, EY, VB, WI, UP, DN, EXL, EYL = range(8)
RHS = 4
GHOST = 8
TILE = 8
LANES = 128


def rows_at(tile):
    return pl.ds(pl.multiple_of(tile * TILE, TILE), TILE)


def kernel(
    axes, table, vn, vp, cap, ex, ey, vb, ids, placed, xo, ro,
    pack, recv, coef, s_buf, u_buf, ysend, yrecv, cur, part, gath, packo, recvo,
    t_ss, t_rs, l_s, x_ss, x_rs, y_ss, y_rs, r_ss, r_rs, o_ss, o_rs, lo_s,
):
    n_gx, n_gy, n_al = axes
    gx, gy, al = lax.axis_index("gx"), lax.axis_index("gy"), lax.axis_index("al")
    group, cols, rows = vn.shape
    layers = group * n_al
    width = rows // n_al
    half = cols // 2
    half_tiles = half // TILE
    own_tiles = cols // TILE
    tiles = own_tiles + 2
    odd = gy % 2
    strip = al * (1 - odd) + (n_al - 1 - al) * odd
    turn = 1 - 2 * odd

    def home(j):
        return j * (1 - odd) + (n_al - 1 - j) * odd

    at_hi = strip // (n_al - 1)
    at_lo = (n_al - 1 - strip) // (n_al - 1)
    right = {"gy": (gy + at_hi) % n_gy, "al": al + turn * (1 - at_hi)}
    left = {"gy": (gy + (n_gy - 1) * at_lo) % n_gy, "al": al - turn * (1 - at_lo)}
    fore = {"gx": (gx + 1) % n_gx}
    back = {"gx": (gx + n_gx - 1) % n_gx}
    al_peers = [{"al": (al + k) % n_al} for k in range(1, n_al)]
    gx_peers = [{"gx": (gx + k) % n_gx} for k in range(1, n_gx)]
    gy_peers = [{"gy": (gy + k) % n_gy} for k in range(1, n_gy)]
    sum_groups = (gx_peers, gy_peers, al_peers)

    barrier = pltpu.get_barrier_semaphore()
    for peer in al_peers + gx_peers + gy_peers:
        pl.semaphore_signal(barrier, inc=1, device_id=peer, device_id_type=MESH)
    pl.semaphore_wait(barrier, len(al_peers + gx_peers + gy_peers))

    lane = lax.broadcasted_iota(jnp.int32, (TILE, LANES), 1)
    sub = lax.broadcasted_iota(jnp.int32, (TILE, LANES), 0)
    low = lane < width
    zero = jnp.zeros((TILE, LANES), jnp.float32)

    def value(which, layer, tile, q):
        at = (layer, rows_at(tile), pl.ds(q * LANES, LANES))
        if which == EX:
            last = (gx * cols + tile * TILE + sub) == n_gx * cols - 1
            return jnp.where(last, 0.0, ex[at])
        if which == EY:
            last = (gy * rows + q * LANES + lane) == n_gy * rows - 1
            return jnp.where(last, 0.0, ey[at])
        if which == VB:
            return jnp.where(al * group + layer == 0, 0.0, vb[at])
        if which == WI:
            return cap[at]
        return cap[at] * (4.0 * vn[at] - vp[at]) / 3.0

    def pack_array(which):
        for layer in range(group):
            def one(tile, c):
                for q in range(rows // LANES):
                    lo = value(which, layer, tile, q)
                    hi = value(which, layer, tile + half_tiles, q)
                    pack[which, 2 * q, layer, rows_at(tile)] = jnp.where(low, lo, pltpu.roll(hi, width, 1))
                    pack[which, 2 * q + 1, layer, rows_at(tile)] = jnp.where(low, pltpu.roll(lo, width, 1), hi)
                return c

            lax.fori_loop(0, half_tiles, one, 0)

    def own_copy(which):
        return pltpu.make_async_copy(
            pack.at[which, strip], recv.at[which, pl.ds(group * al, group)], l_s.at[which]
        )

    for which in range(5):
        pack_array(which)
        for k in (4, 3, 5, 2, 6, 1, 7):
            to = (al + k) % n_al
            pltpu.make_async_remote_copy(
                src_ref=pack.at[which, home(to)],
                dst_ref=recv.at[which, pl.ds(group * al, group)],
                send_sem=t_ss.at[which],
                recv_sem=t_rs.at[which],
                device_id={"al": to},
                device_id_type=MESH,
            ).start()
        own_copy(which).start()

    def wait_array(which):
        many = recv.at[which, pl.ds(0, group * (n_al - 1))]
        pltpu.make_async_remote_copy(
            many, many, t_ss.at[which], t_rs.at[which], device_id={"al": al_peers[0]["al"]}, device_id_type=MESH
        ).wait_recv()
        own_copy(which).wait()

    mine = ids.at[:, pl.ds(pl.multiple_of((strip // 2) * LANES, LANES), LANES)]
    mine_placed = placed.at[:, pl.ds(pl.multiple_of((strip // 2) * LANES, LANES), LANES)]

    def stamp(tile, c):
        code = mine[rows_at(tile)]
        total = zero
        for kind in range(table.shape[0]):
            total = jnp.where(code == kind, table[kind], total)
        total = total * mine_placed[rows_at(tile)].astype(jnp.float32)
        total = jnp.where(strip % 2 == 0, total, pltpu.roll(total, width, 1))
        cur[rows_at(tile)] = total
        return c

    lax.fori_loop(0, own_tiles, stamp, 0)

    def unpack(which, dest):
        def one(layer, c):
            for tile in range(half_tiles):
                v = recv[which, layer, rows_at(tile)]
                dest[layer, rows_at(tile + 1)] = jnp.where(low, v, 0.0)
                dest[layer, rows_at(tile + 1 + half_tiles)] = jnp.where(low, pltpu.roll(v, width, 1), 0.0)
            return c

        lax.fori_loop(0, layers, one, 0)

    def x_copies(which, dest):
        down = pltpu.make_async_remote_copy(
            dest.at[:, pl.ds(cols, GHOST)], dest.at[:, pl.ds(0, GHOST)],
            x_ss.at[which, 0], x_rs.at[which, 0], device_id=fore, device_id_type=MESH,
        )
        up = pltpu.make_async_remote_copy(
            dest.at[:, pl.ds(GHOST, GHOST)], dest.at[:, pl.ds(GHOST + cols, GHOST)],
            x_ss.at[which, 1], x_rs.at[which, 1], device_id=back, device_id_type=MESH,
        )
        return down, up

    def y_copies(which):
        out = []
        for way, peer in ((0, right), (1, left)):
            out.append(
                pltpu.make_async_remote_copy(
                    ysend.at[which, way], yrecv.at[which, way],
                    y_ss.at[which, way], y_rs.at[which, way], device_id=peer, device_id_type=MESH,
                )
            )
        return out

    def start_x(which, dest):
        for copy in x_copies(which, dest):
            copy.start()

    def start_y(which, dest):
        for copy in x_copies(which, dest):
            copy.wait()

        def trim(layer, c):
            dest[layer, rows_at(0)] = jnp.where(gx == 0, 0.0, dest[layer, rows_at(0)])
            dest[layer, rows_at(tiles - 1)] = jnp.where(gx == n_gx - 1, 0.0, dest[layer, rows_at(tiles - 1)])
            return c

        lax.fori_loop(0, layers, trim, 0)

        def one(tile, c):
            to_right, to_left = zero, zero
            for layer in range(layers):
                here = lane // GHOST == layer
                v = dest[layer, rows_at(tile)]
                to_right = jnp.where(here, pltpu.roll(v, (GHOST * layer - (width - GHOST)) % LANES, 1), to_right)
                to_left = jnp.where(here, pltpu.roll(v, GHOST * layer, 1), to_left)
            ysend[which, 0, rows_at(tile)] = to_right
            ysend[which, 1, rows_at(tile)] = to_left
            return c

        lax.fori_loop(0, tiles, one, 0)
        for copy in y_copies(which):
            copy.start()

    first = gy * n_al + strip == 0
    final = gy * n_al + strip == n_gy * n_al - 1

    def finish_y(which, dest):
        for copy in y_copies(which):
            copy.wait()

        def one(tile, c):
            from_left = jnp.where(first, 0.0, yrecv[which, 0, rows_at(tile)])
            from_right = jnp.where(final, 0.0, yrecv[which, 1, rows_at(tile)])
            for layer in range(layers):
                v = dest[layer, rows_at(tile)]
                lft = pltpu.roll(from_left, (LANES - GHOST - GHOST * layer) % LANES, 1)
                rgt = pltpu.roll(from_right, (width - GHOST * layer) % LANES, 1)
                edge = jnp.where(lane < width + GHOST, rgt, jnp.where(lane >= LANES - GHOST, lft, 0.0))
                dest[layer, rows_at(tile)] = jnp.where(low, v, edge)
            return c

        lax.fori_loop(0, tiles, one, 0)

    def before(v, previous):
        return pltpu.roll(jnp.where(sub == TILE - 1, previous, v), 1, 0)

    def after(v, following):
        return pltpu.roll(jnp.where(sub == 0, following, v), TILE - 1, 0)

    u0 = u_buf.at[0]
    c_of = [coef.at[i] for i in range(8)]

    wait_array(EX)
    unpack(EX, c_of[EX])
    start_x(EX, c_of[EX])
    wait_array(EY)
    unpack(EY, c_of[EY])
    start_x(EY, c_of[EY])
    start_y(EX, c_of[EX])
    wait_array(VB)
    unpack(VB, c_of[VB])
    start_x(VB, c_of[VB])
    start_y(EY, c_of[EY])
    finish_y(EX, c_of[EX])
    start_y(VB, c_of[VB])
    finish_y(EY, c_of[EY])

    def lefts(tile, c):
        above = jnp.maximum(tile - 1, 0)
        for layer in range(layers):
            coef[EXL, layer, rows_at(tile)] = before(coef[EX, layer, rows_at(tile)], coef[EX, layer, rows_at(above)])
            coef[EYL, layer, rows_at(tile)] = pltpu.roll(coef[EY, layer, rows_at(tile)], 1, 1)
        return c

    lax.fori_loop(0, tiles, lefts, 0)
    finish_y(VB, c_of[VB])
    wait_array(WI)

    def pivots(tile, c):
        at = rows_at(tile + 1)
        upper = tile // half_tiles
        inverse = zero
        for layer in range(layers):
            held = recv[WI, layer, rows_at(tile % half_tiles)]
            held = jnp.where(upper == 0, held, pltpu.roll(held, width, 1))
            below = coef[VB, layer, at]
            diag = held + coef[EX, layer, at] + coef[EXL, layer, at] + coef[EY, layer, at] + coef[EYL, layer, at] + below
            if layer + 1 < layers:
                diag = diag + coef[VB, layer + 1, at]
            if layer:
                diag = diag - below * below * inverse
            inverse = jnp.where(low, 1.0 / diag, 0.0)
            coef[WI, layer, at] = inverse
        return c

    lax.fori_loop(0, own_tiles, pivots, 0)
    start_x(WI, c_of[WI])
    start_y(WI, c_of[WI])
    wait_array(RHS)
    unpack(RHS, u0)

    def add_stamp(tile, c):
        u0[0, rows_at(tile + 1)] = u0[0, rows_at(tile + 1)] + jnp.where(low, cur[rows_at(tile)], 0.0)
        return c

    lax.fori_loop(0, own_tiles, add_stamp, 0)
    start_x(RHS, u0)
    finish_y(WI, c_of[WI])

    def factors(tile, c):
        at = rows_at(tile)
        for layer in range(layers):
            inverse = coef[WI, layer, at]
            coef[UP, layer, at] = coef[VB, layer, at] * inverse
            if layer + 1 < layers:
                coef[DN, layer, at] = coef[VB, layer + 1, at] * inverse
        return c

    lax.fori_loop(0, tiles, factors, 0)
    start_y(RHS, u0)
    finish_y(RHS, u0)

    def solve(us, at):
        kept = []
        d = None
        for layer in range(layers):
            term = us[layer] * coef[WI, layer, at]
            d = term if layer == 0 else term + coef[UP, layer, at] * d
            kept.append(d)
        for layer in range(layers - 2, -1, -1):
            kept[layer] = kept[layer] + coef[DN, layer, at] * kept[layer + 1]
        return kept

    def is_own(tile):
        return jnp.logical_and(tile >= 1, tile <= own_tiles)

    def begin(tile, acc):
        at = rows_at(tile)
        us = [u_buf[0, layer, at] for layer in range(layers)]
        ss = solve(us, at)
        total = zero
        for layer in range(layers):
            s_buf[0, layer, at] = ss[layer]
            total = total + ss[layer] * us[layer]
        return acc + jnp.where(is_own(tile), total, 0.0)

    part[0] = lax.fori_loop(0, tiles, begin, zero)

    def apply(k, onward):
        twice = jnp.where(k == 0, 1.0, 2.0)
        once = jnp.where(k == 0, 0.0, 1.0)
        older = jnp.maximum(k - 1, 0)

        def one(tile, accs):
            at = rows_at(tile)
            above = rows_at(jnp.maximum(tile - 1, 0))
            under = rows_at(jnp.minimum(tile + 1, tiles - 1))
            cross, square = zero, zero
            us = []
            for layer in range(layers):
                v = s_buf[k, layer, at]
                t = coef[EX, layer, at] * after(v, s_buf[k, layer, under])
                t = t + coef[EXL, layer, at] * before(v, s_buf[k, layer, above])
                t = t + coef[EY, layer, at] * pltpu.roll(v, LANES - 1, 1)
                t = t + coef[EYL, layer, at] * pltpu.roll(v, 1, 1)
                u = twice * t - once * u_buf[older, layer, at]
                u_buf[k + 1, layer, at] = u
                cross = cross + v * u
                us.append(u)
            if onward:
                ss = solve(us, at)
                for layer in range(layers):
                    s_buf[k + 1, layer, at] = ss[layer]
                    square = square + ss[layer] * us[layer]
            own = is_own(tile)
            return accs[0] + jnp.where(own, cross, 0.0), accs[1] + jnp.where(own, square, 0.0)

        cross, square = lax.fori_loop(0 if onward else 1, tiles if onward else tiles - 1, one, (zero, zero))
        part[2 * k + 1] = cross
        if onward:
            part[2 * k + 2] = square

    def steps(k, c):
        apply(k, True)
        return c

    lax.fori_loop(0, ITERS - 1, steps, 0)
    apply(ITERS - 1, False)

    n_sums = 2 * ITERS
    gath[0, 0] = jnp.sum(jnp.where(low[None], part[...], 0.0), axis=1)
    for stage, peers in enumerate(sum_groups):
        for slot, peer in enumerate(peers):
            pltpu.make_async_remote_copy(
                gath.at[stage, 0], gath.at[stage, slot + 1], r_ss.at[stage], r_rs.at[stage],
                device_id=peer, device_id_type=MESH,
            ).start()
        many = gath.at[stage, pl.ds(1, len(peers))]
        pltpu.make_async_remote_copy(
            many, many, r_ss.at[stage], r_rs.at[stage], device_id=peers[0], device_id_type=MESH
        ).wait()
        gath[stage + 1, 0] = jnp.sum(gath[stage, 0 : len(peers) + 1], axis=0)
    sums = jnp.broadcast_to(jnp.sum(gath[len(sum_groups), 0], axis=1, keepdims=True), (n_sums, LANES))
    pair = [sums[i : i + 1] for i in range(n_sums)]
    moment = [pair[0], pair[1]]
    for i in range(2, n_sums):
        moment.append(2.0 * pair[i] - pair[i % 2])
    q = [moment[0] - moment[1]]
    for i in range(1, n_sums - 1):
        q.append(moment[i] - 0.5 * (moment[i + 1] + moment[i - 1]))
    mat = [[0.5 * (q[i + j] + q[abs(i - j)]) for j in range(ITERS)] for i in range(ITERS)]
    vec = [moment[i] for i in range(ITERS)]
    inv = []
    for k in range(ITERS):
        inv.append(1.0 / mat[k][k])
        for i in range(k + 1, ITERS):
            ratio = mat[k][i] * inv[k]
            for j in range(i, ITERS):
                mat[i][j] = mat[i][j] - ratio * mat[k][j]
            vec[i] = vec[i] - ratio * vec[k]
    c = [None] * ITERS
    for k in range(ITERS - 1, -1, -1):
        total = vec[k]
        for j in range(k + 1, ITERS):
            total = total - mat[k][j] * c[j]
        c[k] = total * inv[k]
    e = []
    for n in range(ITERS + 1):
        total = jnp.ones_like(c[0]) if n == 0 else jnp.zeros_like(c[0])
        if n < ITERS:
            total = total - c[n]
        if n >= 1:
            total = total + (1.0 if n == 1 else 0.5) * c[n - 1]
        if n + 1 < ITERS:
            total = total + 0.5 * c[n + 1]
        e.append(total)
    cs = [jnp.broadcast_to(a, (TILE, LANES)) for a in c]
    es = [jnp.broadcast_to(a, (TILE, LANES)) for a in e]

    def out_copy(which, to):
        return pltpu.make_async_remote_copy(
            packo.at[which, to], recvo.at[which, strip], o_ss.at[which], o_rs.at[which],
            device_id={"al": to}, device_id_type=MESH,
        )

    def combine(buf, weights, layer, tile):
        at = rows_at(tile)
        total = weights[0] * buf[0, layer, at]
        for j in range(1, len(weights)):
            total = total + weights[j] * buf[j, layer, at]
        return total

    for k in (4, 3, 5, 2, 6, 1, 7, 0):
        to = (al + k) % n_al
        for which, buf, weights in ((0, s_buf, cs), (1, u_buf, es)):
            for member in range(group):
                layer = to * group + member

                def one(tile, carry):
                    lo = combine(buf, weights, layer, tile + 1)
                    hi = combine(buf, weights, layer, tile + 1 + half_tiles)
                    packo[which, to, member, rows_at(tile)] = jnp.where(low, lo, pltpu.roll(hi, width, 1))
                    return carry

                lax.fori_loop(0, half_tiles, one, 0)
            if k:
                out_copy(which, to).start()
            else:
                pltpu.make_async_copy(packo.at[which, al], recvo.at[which, strip], lo_s.at[which]).start()

    for which, dest in ((0, xo), (1, ro)):
        many = recvo.at[which, pl.ds(0, n_al - 1)]
        pltpu.make_async_remote_copy(
            many, many, o_ss.at[which], o_rs.at[which], device_id=al_peers[0], device_id_type=MESH
        ).wait()
        pltpu.make_async_copy(packo.at[which, al], recvo.at[which, strip], lo_s.at[which]).wait()

        def one(tile, carry):
            for member in range(group):
                for tq in range(rows // LANES):
                    p = recvo[which, 2 * tq, member, rows_at(tile)]
                    r = recvo[which, 2 * tq + 1, member, rows_at(tile)]
                    dest[member, rows_at(tile), pl.ds(tq * LANES, LANES)] = jnp.where(low, p, pltpu.roll(r, width, 1))
                    dest[member, rows_at(tile + half_tiles), pl.ds(tq * LANES, LANES)] = jnp.where(
                        low, pltpu.roll(p, width, 1), r
                    )
            return carry

        lax.fori_loop(0, half_tiles, one, 0)

    for which in range(5):
        many = recv.at[which, pl.ds(0, group * (n_al - 1))]
        pltpu.make_async_remote_copy(
            many, many, t_ss.at[which], t_rs.at[which], device_id=al_peers[0], device_id_type=MESH
        ).wait_send()


def solution(mesh):
    axes = (mesh.shape["gx"], mesh.shape["gy"], mesh.shape["al"])

    def block(volt_now, volt_prev, cap_term, edge_x, edge_y, via_below, cell_ids, placed, current_table):
        group, cols, rows = volt_now.shape
        layers = group * axes[2]
        tall = cols + 2 * GHOST
        dma = pltpu.SemaphoreType.DMA
        f32 = jnp.float32
        return pl.pallas_call(
            functools.partial(kernel, axes),
            out_shape=(jax.ShapeDtypeStruct(volt_now.shape, f32),) * 2,
            in_specs=[pl.BlockSpec(memory_space=pltpu.SMEM)] + [pl.BlockSpec(memory_space=pltpu.VMEM)] * 8,
            out_specs=(pl.BlockSpec(memory_space=pltpu.VMEM),) * 2,
            scratch_shapes=[
                pltpu.VMEM((5, axes[2], group, cols // 2, LANES), f32),
                pltpu.VMEM((5, layers, cols // 2, LANES), f32),
                pltpu.VMEM((8, layers, tall, LANES), f32),
                pltpu.VMEM((ITERS, layers, tall, LANES), f32),
                pltpu.VMEM((ITERS + 1, layers, tall, LANES), f32),
                pltpu.VMEM((5, 2, tall, LANES), f32),
                pltpu.VMEM((5, 2, tall, LANES), f32),
                pltpu.VMEM((cols, LANES), f32),
                pltpu.VMEM((2 * ITERS, TILE, LANES), f32),
                pltpu.VMEM((4, max(axes), 2 * ITERS, LANES), f32),
                pltpu.VMEM((2, axes[2], group, cols // 2, LANES), f32),
                pltpu.VMEM((2, axes[2], group, cols // 2, LANES), f32),
                dma((5,)), dma((5,)), dma((5,)),
                dma((5, 2)), dma((5, 2)), dma((5, 2)), dma((5, 2)),
                dma((3,)), dma((3,)), dma((2,)), dma((2,)), dma((2,)),
            ],
            compiler_params=pltpu.CompilerParams(
                collective_id=0, has_side_effects=True, vmem_limit_bytes=48 << 20
            ),
        )(current_table, volt_now, volt_prev, cap_term, edge_x, edge_y, via_below, cell_ids, placed)

    spec = P("al", "gx", "gy")
    return jax.shard_map(
        block,
        mesh=mesh,
        in_specs=(spec,) * 6 + (P("gx", "gy"), P("gx", "gy"), P()),
        out_specs=(spec, spec),
        check_vma=False,
    )
```

time: 2470 us -> 119 us (0.05)
  blocking collectives: 1150 us -> 0 us
  waiting for transfers between devices: 940 us -> 0 us
  other arithmetic: 166 us -> 0 us
  starting transfers between devices: 144 us -> 0 us
  Pallas kernels: 0 us -> 108 us
  between operations: 36.1 us -> 0.66 us
    psum x15 -> x0, blocking collectives: 1150 us -> none  [the longest x8 629 us: inner_sum(): return lax.psum(jnp.sum(resid * zvec), ('gx', 'gy', 'al'))]
    all_gather x22 -> x0, waiting for transfers between devices: 847 us -> none  [carried_in(): gathered = jax.tree.map(lambda a: lax.all_gather(a, axis), part)]
    ppermute x53 -> x0, starting transfers between devices: 143 us -> none  [the longest x26 90.9 us: extended(): lax.ppermute(tail, axis, [(i, (i + 1) % count) for i in range(ends)])]
    add x81 -> x0, other arithmetic: 113 us -> none  [the longest x56 83.2 us: affine_join(): return (earlier[0] * later[0], later[0] * earlier[1] + later[1])]
    pallas_call x0 -> x1, Pallas kernels: none -> 108 us  [block(): pl.pallas_call(functools.partial(kernel, axes), out_shape=(jax.ShapeDtype...]
    ppermute x53 -> x0, waiting for transfers between devices: 90.5 us -> none  [the longest x27 57.9 us: extended(): lax.ppermute(head, axis, [((i + 1) % count, i) for i in range(ends)])]
  transfers between devices with their start and end apart: 75 -> 0, of which waited for: 66 -> 0; matrix products, arithmetic and copies ran while one was open for 0% -> 0% of each run, Pallas kernels for 0% -> 0%
where the time goes in v1:
time: 119 us
  Pallas kernels  108 us (91%)
  local copies, waits for them, and re-layouts  9.56 us (8%)
    pallas_call x1, Pallas kernels, block(): pl.pallas_call(functools.partial(kernel, axes), out_shape=(jax.ShapeDtype...  108 us
    unnamed x20, local copies, waits for them, and re-layouts  9.56 us

profile of v1, /device:TPU:1, one launch (start us, length us, event | category | flops | bytes accessed | tf_op | source)
XLA Modules:
  0.0 118.7 jit_solution(5304690390341054404)
XLA Ops:
  0.6 0.0 copy-start
  0.6 0.9 copy-done
  1.6 0.0 copy-start.1
  1.6 0.9 copy-done.1
  2.5 0.0 copy-start.2
  2.5 0.9 copy-done.2
  3.5 0.0 copy-start.3
  3.5 0.9 copy-done.3
  4.4 0.0 copy-start.4
  4.4 0.9 copy-done.4
  5.4 0.0 copy-start.5
  5.4 0.9 copy-done.5
  6.3 0.0 copy-start.6
  6.3 0.9 copy-done.6
  7.2 0.0 copy-start.7
  7.2 0.9 copy-done.7
  8.1 0.0 copy-start.8
  8.1 0.7 copy-done.8
  8.8 108.5 %shard_map.104 = (f32[2,64,512]{2,1,0:T(8,128)S(1)}, f32[2,64,512]{2,1,0:T(8,128)S(1)}) custom-call(f32[64]{0:T(128)S(1)} %copy-done.8, f32[2,64,512]{2,1,0:T(8,128)S(1)} %copy-done, f32[2,64,512]{2,1,0:T(8,128)S(1)} %copy-done.1, f32[2,64,512]{2,1,0:T(8,128)S(1)} %copy-done.2, f32[2,64,512]{2,1,0:T(8,128)S(1)} %copy-done.3, f32[2,64,512]{2,1,0:T(8,128)S(1)} %copy-done.4, ...), custom_call_target="tpu_custom_call" | custom-call | tf_op jit(solution)/shard_map/pallas_call | solution.py:477
  117.3 0.7 copy.13
  118.0 0.7 copy.14
Async XLA Ops:
  0.6 1.0 copy-start
  1.6 0.9 copy-start.1
  2.5 0.9 copy-start.2
  3.5 0.9 copy-start.3
  4.4 0.9 copy-start.4
  5.4 0.9 copy-start.5
  6.3 0.9 copy-start.6
  7.2 0.9 copy-start.7
  8.1 0.7 copy-start.8

commit v2 on v1

--- a/solution.py
+++ b/solution.py
@@ -14,15 +14,53 @@
 GHOST = 8
 TILE = 8
 LANES = 128
+AT_ONCE = 2
+REFINE = 3
 
 
 def rows_at(tile):
     return pl.ds(pl.multiple_of(tile * TILE, TILE), TILE)
 
 
+def two_sum(a, b):
+    s = a + b
+    t = s - a
+    return s, (a - (s - t)) + (b - t)
+
+
+def pair_add(a, b):
+    s, t = two_sum(a[0], b[0])
+    t = t + (a[1] + b[1])
+    high = s + t
+    return high, t - (high - s)
+
+
+def pair_less(a, b):
+    return pair_add(a, (-b[0], -b[1]))
+
+
+def scaled(power, a):
+    return power * a[0], power * a[1]
+
+
+def cut(a):
+    t = 4097.0 * a
+    high = t - (t - a)
+    return high, a - high
+
+
+def pair_times(a, b):
+    p = a[0] * b[0]
+    (ah, al), (bh, bl) = cut(a[0]), cut(b[0])
+    t = ((ah * bh - p) + ah * bl + al * bh) + al * bl
+    t = t + (a[0] * b[1] + a[1] * b[0])
+    high = p + t
+    return high, t - (high - p)
+
+
 def kernel(
-    axes, table, vn, vp, cap, ex, ey, vb, ids, placed, xo, ro,
-    pack, recv, coef, s_buf, u_buf, ysend, yrecv, cur, part, gath, packo, recvo,
+    axes, table, vn_h, vp_h, cap_h, ex_h, ey_h, vb_h, ids_h, placed_h, xo, ro,
+    vn, vp, cap, ex, ey, vb, ids, placed, in_s, pack, recv, coef, s_buf, u_buf, ysend, yrecv, cur, part, gath, packo, recvo,
     t_ss, t_rs, l_s, x_ss, x_rs, y_ss, y_rs, r_ss, r_rs, o_ss, o_rs, lo_s,
 ):
     n_gx, n_gy, n_al = axes
@@ -47,15 +85,29 @@
     left = {"gy": (gy + (n_gy - 1) * at_lo) % n_gy, "al": al - turn * (1 - at_lo)}
     fore = {"gx": (gx + 1) % n_gx}
     back = {"gx": (gx + n_gx - 1) % n_gx}
-    al_peers = [{"al": (al + k) % n_al} for k in range(1, n_al)]
-    gx_peers = [{"gx": (gx + k) % n_gx} for k in range(1, n_gx)]
-    gy_peers = [{"gy": (gy + k) % n_gy} for k in range(1, n_gy)]
-    sum_groups = (gx_peers, gy_peers, al_peers)
+    al_peers = [{"al": (al + k) % n_al} for k in (4, 3, 5, 2, 6, 1, 7)]
+    plane_peers = [
+        {"gx": (gx + i) % n_gx, "gy": (gy + j) % n_gy}
+        for i in (4, 5, 3, 2, 6, 7, 1, 0) for j in (2, 1, 3, 0) if i or j
+    ]
+    sum_groups = (plane_peers, al_peers)
+    everyone = al_peers + plane_peers
+    diagonal = [
+        {"gx": (gx + i) % n_gx, "al": (al + j) % n_al} for i in (1, n_gx - 1) for j in (1, n_al - 1)
+    ]
 
     barrier = pltpu.get_barrier_semaphore()
-    for peer in al_peers + gx_peers + gy_peers:
+    for peer in everyone + diagonal:
         pl.semaphore_signal(barrier, inc=1, device_id=peer, device_id_type=MESH)
-    pl.semaphore_wait(barrier, len(al_peers + gx_peers + gy_peers))
+    reads = {
+        name: pltpu.make_async_copy(src, dst, in_s.at[i])
+        for i, (name, src, dst) in enumerate((
+            (EX, ex_h, ex), (EY, ey_h, ey), (VB, vb_h, vb), (WI, cap_h, cap),
+            ("vn", vn_h, vn), ("vp", vp_h, vp), ("ids", ids_h, ids), ("placed", placed_h, placed),
+        ))
+    }
+    for copy in reads.values():
+        copy.start()
 
     lane = lax.broadcasted_iota(jnp.int32, (TILE, LANES), 1)
     sub = lax.broadcasted_iota(jnp.int32, (TILE, LANES), 0)
@@ -93,8 +145,17 @@
             pack.at[which, strip], recv.at[which, pl.ds(group * al, group)], l_s.at[which]
         )
 
+    reads[EX].wait()
+    pack_array(EX)
+    pl.semaphore_wait(barrier, len(everyone + diagonal))
     for which in range(5):
-        pack_array(which)
+        if which in (EY, VB, WI):
+            reads[which].wait()
+        if which == RHS:
+            reads["vn"].wait()
+            reads["vp"].wait()
+        if which != EX:
+            pack_array(which)
         for k in (4, 3, 5, 2, 6, 1, 7):
             to = (al + k) % n_al
             pltpu.make_async_remote_copy(
@@ -124,20 +185,27 @@
             total = jnp.where(code == kind, table[kind], total)
         total = total * mine_placed[rows_at(tile)].astype(jnp.float32)
         total = jnp.where(strip % 2 == 0, total, pltpu.roll(total, width, 1))
-        cur[rows_at(tile)] = total
+        cur[rows_at(tile)] = jnp.where(low, total, 0.0)
         return c
 
+    reads["ids"].wait()
+    reads["placed"].wait()
     lax.fori_loop(0, own_tiles, stamp, 0)
 
     def unpack(which, dest):
-        def one(layer, c):
-            for tile in range(half_tiles):
+        def one(tile, c):
+            for layer in range(layers):
                 v = recv[which, layer, rows_at(tile)]
-                dest[layer, rows_at(tile + 1)] = jnp.where(low, v, 0.0)
-                dest[layer, rows_at(tile + 1 + half_tiles)] = jnp.where(low, pltpu.roll(v, width, 1), 0.0)
+                lo = jnp.where(low, v, 0.0)
+                hi = jnp.where(low, pltpu.roll(v, width, 1), 0.0)
+                if which == RHS and layer == 0:
+                    lo = lo + cur[rows_at(tile)]
+                    hi = hi + cur[rows_at(tile + half_tiles)]
+                dest[layer, rows_at(tile + 1)] = lo
+                dest[layer, rows_at(tile + 1 + half_tiles)] = hi
             return c
 
-        lax.fori_loop(0, layers, one, 0)
+        lax.fori_loop(0, half_tiles, one, 0)
 
     def x_copies(which, dest):
         down = pltpu.make_async_remote_copy(
@@ -153,28 +221,23 @@
     def y_copies(which):
         out = []
         for way, peer in ((0, right), (1, left)):
-            out.append(
-                pltpu.make_async_remote_copy(
-                    ysend.at[which, way], yrecv.at[which, way],
-                    y_ss.at[which, way], y_rs.at[which, way], device_id=peer, device_id_type=MESH,
+            for part_of, across, src, dst in (
+                (0, {}, pl.ds(GHOST, cols), pl.ds(GHOST, cols)),
+                (1, fore, pl.ds(cols, GHOST), pl.ds(0, GHOST)),
+                (2, back, pl.ds(GHOST, GHOST), pl.ds(GHOST + cols, GHOST)),
+            ):
+                out.append(
+                    pltpu.make_async_remote_copy(
+                        ysend.at[which, way, src], yrecv.at[which, way, dst],
+                        y_ss.at[which, way, part_of], y_rs.at[which, way, part_of],
+                        device_id={**peer, **across}, device_id_type=MESH,
+                    )
                 )
-            )
         return out
 
-    def start_x(which, dest):
+    def start_edges(which, dest):
         for copy in x_copies(which, dest):
             copy.start()
-
-    def start_y(which, dest):
-        for copy in x_copies(which, dest):
-            copy.wait()
-
-        def trim(layer, c):
-            dest[layer, rows_at(0)] = jnp.where(gx == 0, 0.0, dest[layer, rows_at(0)])
-            dest[layer, rows_at(tiles - 1)] = jnp.where(gx == n_gx - 1, 0.0, dest[layer, rows_at(tiles - 1)])
-            return c
-
-        lax.fori_loop(0, layers, trim, 0)
 
         def one(tile, c):
             to_right, to_left = zero, zero
@@ -187,18 +250,23 @@
             ysend[which, 1, rows_at(tile)] = to_left
             return c
 
-        lax.fori_loop(0, tiles, one, 0)
+        lax.fori_loop(1, own_tiles + 1, one, 0)
         for copy in y_copies(which):
             copy.start()
 
     first = gy * n_al + strip == 0
     final = gy * n_al + strip == n_gy * n_al - 1
 
-    def finish_y(which, dest):
+    def finish_edges(which, dest):
+        for copy in x_copies(which, dest):
+            copy.wait()
         for copy in y_copies(which):
             copy.wait()
 
         def one(tile, c):
+            outside = jnp.logical_or(
+                jnp.logical_and(gx == 0, tile == 0), jnp.logical_and(gx == n_gx - 1, tile == tiles - 1)
+            )
             from_left = jnp.where(first, 0.0, yrecv[which, 0, rows_at(tile)])
             from_right = jnp.where(final, 0.0, yrecv[which, 1, rows_at(tile)])
             for layer in range(layers):
@@ -206,7 +274,7 @@
                 lft = pltpu.roll(from_left, (LANES - GHOST - GHOST * layer) % LANES, 1)
                 rgt = pltpu.roll(from_right, (width - GHOST * layer) % LANES, 1)
                 edge = jnp.where(lane < width + GHOST, rgt, jnp.where(lane >= LANES - GHOST, lft, 0.0))
-                dest[layer, rows_at(tile)] = jnp.where(low, v, edge)
+                dest[layer, rows_at(tile)] = jnp.where(outside, 0.0, jnp.where(low, v, edge))
             return c
 
         lax.fori_loop(0, tiles, one, 0)
@@ -220,20 +288,12 @@
     u0 = u_buf.at[0]
     c_of = [coef.at[i] for i in range(8)]
 
-    wait_array(EX)
-    unpack(EX, c_of[EX])
-    start_x(EX, c_of[EX])
-    wait_array(EY)
-    unpack(EY, c_of[EY])
-    start_x(EY, c_of[EY])
-    start_y(EX, c_of[EX])
-    wait_array(VB)
-    unpack(VB, c_of[VB])
-    start_x(VB, c_of[VB])
-    start_y(EY, c_of[EY])
-    finish_y(EX, c_of[EX])
-    start_y(VB, c_of[VB])
-    finish_y(EY, c_of[EY])
+    for which in (EX, EY, VB):
+        wait_array(which)
+        unpack(which, c_of[which])
+        start_edges(which, c_of[which])
+    finish_edges(EX, c_of[EX])
+    finish_edges(EY, c_of[EY])
 
     def lefts(tile, c):
         above = jnp.maximum(tile - 1, 0)
@@ -243,7 +303,6 @@
         return c
 
     lax.fori_loop(0, tiles, lefts, 0)
-    finish_y(VB, c_of[VB])
     wait_array(WI)
 
     def pivots(tile, c):
@@ -264,18 +323,12 @@
         return c
 
     lax.fori_loop(0, own_tiles, pivots, 0)
-    start_x(WI, c_of[WI])
-    start_y(WI, c_of[WI])
+    start_edges(WI, c_of[WI])
+    finish_edges(VB, c_of[VB])
     wait_array(RHS)
     unpack(RHS, u0)
-
-    def add_stamp(tile, c):
-        u0[0, rows_at(tile + 1)] = u0[0, rows_at(tile + 1)] + jnp.where(low, cur[rows_at(tile)], 0.0)
-        return c
-
-    lax.fori_loop(0, own_tiles, add_stamp, 0)
-    start_x(RHS, u0)
-    finish_y(WI, c_of[WI])
+    start_edges(RHS, u0)
+    finish_edges(WI, c_of[WI])
 
     def factors(tile, c):
         at = rows_at(tile)
@@ -287,8 +340,7 @@
         return c
 
     lax.fori_loop(0, tiles, factors, 0)
-    start_y(RHS, u0)
-    finish_y(RHS, u0)
+    finish_edges(RHS, u0)
 
     def solve(us, at):
         kept = []
@@ -304,48 +356,60 @@
     def is_own(tile):
         return jnp.logical_and(tile >= 1, tile <= own_tiles)
 
-    def begin(tile, acc):
-        at = rows_at(tile)
-        us = [u_buf[0, layer, at] for layer in range(layers)]
-        ss = solve(us, at)
-        total = zero
-        for layer in range(layers):
-            s_buf[0, layer, at] = ss[layer]
-            total = total + ss[layer] * us[layer]
-        return acc + jnp.where(is_own(tile), total, 0.0)
-
-    part[0] = lax.fori_loop(0, tiles, begin, zero)
+    def begin(turn_at, acc):
+        for step in range(AT_ONCE):
+            tile = turn_at * AT_ONCE + step
+            at = rows_at(tile)
+            us = [u_buf[0, layer, at] for layer in range(layers)]
+            ss = solve(us, at)
+            total = zero
+            for layer in range(layers):
+                s_buf[0, layer, at] = ss[layer]
+                total = total + ss[layer] * us[layer]
+            acc = acc + jnp.where(is_own(tile), total, 0.0)
+        return acc
+
+    part[0] = lax.fori_loop(0, tiles // AT_ONCE, begin, zero)
 
     def apply(k, onward):
         twice = jnp.where(k == 0, 1.0, 2.0)
         once = jnp.where(k == 0, 0.0, 1.0)
         older = jnp.maximum(k - 1, 0)
 
-        def one(tile, accs):
-            at = rows_at(tile)
-            above = rows_at(jnp.maximum(tile - 1, 0))
-            under = rows_at(jnp.minimum(tile + 1, tiles - 1))
-            cross, square = zero, zero
-            us = []
+        def one(turn_at, accs):
+            base = turn_at * AT_ONCE + (0 if onward else 1)
+            ats = [rows_at(base + step) for step in range(AT_ONCE)]
+            above = rows_at(jnp.maximum(base - 1, 0))
+            under = rows_at(jnp.minimum(base + AT_ONCE, tiles - 1))
+            cross = [zero] * AT_ONCE
+            square = [zero] * AT_ONCE
+            us = [[] for _ in ats]
             for layer in range(layers):
-                v = s_buf[k, layer, at]
-                t = coef[EX, layer, at] * after(v, s_buf[k, layer, under])
-                t = t + coef[EXL, layer, at] * before(v, s_buf[k, layer, above])
-                t = t + coef[EY, layer, at] * pltpu.roll(v, LANES - 1, 1)
-                t = t + coef[EYL, layer, at] * pltpu.roll(v, 1, 1)
-                u = twice * t - once * u_buf[older, layer, at]
-                u_buf[k + 1, layer, at] = u
-                cross = cross + v * u
-                us.append(u)
+                vs = [s_buf[k, layer, at] for at in [above] + ats + [under]]
+                for step, at in enumerate(ats):
+                    v = vs[step + 1]
+                    t = coef[EX, layer, at] * after(v, vs[step + 2]) + coef[EXL, layer, at] * before(v, vs[step])
+                    t = t + (
+                        coef[EY, layer, at] * pltpu.roll(v, LANES - 1, 1) + coef[EYL, layer, at] * pltpu.roll(v, 1, 1)
+                    )
+                    u = twice * t - once * u_buf[older, layer, at]
+                    u_buf[k + 1, layer, at] = u
+                    cross[step] = cross[step] + v * u
+                    us[step].append(u)
             if onward:
-                ss = solve(us, at)
-                for layer in range(layers):
-                    s_buf[k + 1, layer, at] = ss[layer]
-                    square = square + ss[layer] * us[layer]
-            own = is_own(tile)
-            return accs[0] + jnp.where(own, cross, 0.0), accs[1] + jnp.where(own, square, 0.0)
-
-        cross, square = lax.fori_loop(0 if onward else 1, tiles if onward else tiles - 1, one, (zero, zero))
+                for step, at in enumerate(ats):
+                    ss = solve(us[step], at)
+                    for layer in range(layers):
+                        s_buf[k + 1, layer, at] = ss[layer]
+                        square[step] = square[step] + ss[layer] * us[step][layer]
+            first_sum, second_sum = accs
+            for step in range(AT_ONCE):
+                own = is_own(base + step)
+                first_sum = first_sum + jnp.where(own, cross[step], 0.0)
+                second_sum = second_sum + jnp.where(own, square[step], 0.0)
+            return first_sum, second_sum
+
+        cross, square = lax.fori_loop(0, (tiles if onward else own_tiles) // AT_ONCE, one, (zero, zero))
         part[2 * k + 1] = cross
         if onward:
             part[2 * k + 2] = square
@@ -358,54 +422,120 @@
     apply(ITERS - 1, False)
 
     n_sums = 2 * ITERS
-    gath[0, 0] = jnp.sum(jnp.where(low[None], part[...], 0.0), axis=1)
+    rowed = lax.broadcasted_iota(jnp.int32, (n_sums, LANES), 0)
+    laned = lax.broadcasted_iota(jnp.int32, (n_sums, LANES), 1)
+
+    def halved(high, low_part, axis):
+        while high.shape[axis] > 1:
+            n = high.shape[axis] // 2
+            a = lax.slice_in_dim(high, 0, n, axis=axis), lax.slice_in_dim(low_part, 0, n, axis=axis)
+            b = lax.slice_in_dim(high, n, 2 * n, axis=axis), lax.slice_in_dim(low_part, n, 2 * n, axis=axis)
+            high, low_part = pair_add(a, b)
+        return high, low_part
+
+    def turned(high, low_part, length, axis):
+        shift = length // 2
+        while shift:
+            high, low_part = pair_add(
+                (high, low_part), (pltpu.roll(high, shift, axis), pltpu.roll(low_part, shift, axis))
+            )
+            shift //= 2
+        return high, low_part
+
+    total = halved(*[jnp.where(low[None], part[...], 0.0), jnp.zeros_like(part)], 1)
+    total = turned(total[0][:, 0], total[1][:, 0], LANES, 1)
+    here = laned == rowed
+    line = jnp.sum(jnp.where(here, total[0], 0.0), axis=0, keepdims=True) + jnp.sum(
+        jnp.where(laned == rowed + LANES // 2, total[1], 0.0), axis=0, keepdims=True
+    )
     for stage, peers in enumerate(sum_groups):
+        count = len(peers) + 1
+        gath[stage, pl.ds(count - 1, 1)] = line
         for slot, peer in enumerate(peers):
             pltpu.make_async_remote_copy(
-                gath.at[stage, 0], gath.at[stage, slot + 1], r_ss.at[stage], r_rs.at[stage],
+                gath.at[stage, pl.ds(count - 1, 1)], gath.at[stage, pl.ds(slot, 1)], r_ss.at[stage], r_rs.at[stage],
                 device_id=peer, device_id_type=MESH,
             ).start()
-        many = gath.at[stage, pl.ds(1, len(peers))]
+        many = gath.at[stage, pl.ds(0, count - 1)]
         pltpu.make_async_remote_copy(
             many, many, r_ss.at[stage], r_rs.at[stage], device_id=peers[0], device_id_type=MESH
         ).wait()
-        gath[stage + 1, 0] = jnp.sum(gath[stage, 0 : len(peers) + 1], axis=0)
-    sums = jnp.broadcast_to(jnp.sum(gath[len(sum_groups), 0], axis=1, keepdims=True), (n_sums, LANES))
-    pair = [sums[i : i + 1] for i in range(n_sums)]
+        got = gath[stage, 0:count]
+        got_low = pltpu.roll(got, LANES // 2, 1)
+        high, low_part = got[0:TILE], got_low[0:TILE]
+        for i in range(1, count // TILE):
+            high, low_part = pair_add(
+                (high, low_part), (got[i * TILE : (i + 1) * TILE], got_low[i * TILE : (i + 1) * TILE])
+            )
+        high, low_part = turned(high, low_part, TILE, 0)
+        line = jnp.where(low, high, pltpu.roll(low_part, LANES // 2, 1))[0:1]
+    spread = jnp.broadcast_to(line, (n_sums, LANES))
+    highs = jnp.broadcast_to(jnp.sum(jnp.where(here, spread, 0.0), axis=1, keepdims=True), (n_sums, LANES))
+    lows = jnp.broadcast_to(
+        jnp.sum(jnp.where(laned == rowed + LANES // 2, spread, 0.0), axis=1, keepdims=True), (n_sums, LANES)
+    )
+
+    def splat(array, i):
+        return jnp.broadcast_to(array[i : i + 1], (TILE, LANES))
+
+    pair = [(splat(highs, i), splat(lows, i)) for i in range(n_sums)]
     moment = [pair[0], pair[1]]
     for i in range(2, n_sums):
-        moment.append(2.0 * pair[i] - pair[i % 2])
-    q = [moment[0] - moment[1]]
+        moment.append(pair_less(scaled(2.0, pair[i]), pair[i % 2]))
+    q = [pair_less(moment[0], moment[1])]
     for i in range(1, n_sums - 1):
-        q.append(moment[i] - 0.5 * (moment[i + 1] + moment[i - 1]))
-    mat = [[0.5 * (q[i + j] + q[abs(i - j)]) for j in range(ITERS)] for i in range(ITERS)]
-    vec = [moment[i] for i in range(ITERS)]
-    inv = []
+        q.append(pair_less(moment[i], scaled(0.5, pair_add(moment[i + 1], moment[i - 1]))))
+
+    def stacked(parts):
+        out = parts[0]
+        for i in range(1, ITERS):
+            out = jnp.where(sub == i, parts[i], out)
+        return out
+
+    def column(j, which):
+        return stacked([q[i + j][which] for i in range(ITERS)]), stacked([q[abs(i - j)][which] for i in range(ITERS)])
+
+    mat = []
+    for j in range(ITERS):
+        (high_a, high_b), (low_a, low_b) = column(j, 0), column(j, 1)
+        mat.append(scaled(0.5, pair_add((high_a, low_a), (high_b, low_b))))
+    vec = (stacked([moment[i][0] for i in range(ITERS)]), stacked([moment[i][1] for i in range(ITERS)]))
+
+    left_over = [m[0] for m in mat]
+    lower, inv = [], []
     for k in range(ITERS):
-        inv.append(1.0 / mat[k][k])
-        for i in range(k + 1, ITERS):
-            ratio = mat[k][i] * inv[k]
-            for j in range(i, ITERS):
-                mat[i][j] = mat[i][j] - ratio * mat[k][j]
-            vec[i] = vec[i] - ratio * vec[k]
-    c = [None] * ITERS
-    for k in range(ITERS - 1, -1, -1):
-        total = vec[k]
+        inv.append(1.0 / splat(left_over[k], k))
+        lower.append(jnp.where(sub > k, left_over[k] * inv[k], 0.0))
         for j in range(k + 1, ITERS):
-            total = total - mat[k][j] * c[j]
-        c[k] = total * inv[k]
+            left_over[j] = left_over[j] - lower[k] * splat(left_over[j], k)
+
+    def solved(right_side):
+        for k in range(ITERS - 1):
+            right_side = right_side - lower[k] * splat(right_side, k)
+        out = [None] * ITERS
+        for k in range(ITERS - 1, -1, -1):
+            out[k] = splat(right_side, k) * inv[k]
+            right_side = right_side - jnp.where(sub < k, left_over[k], 0.0) * out[k]
+        return out
+
+    c = [(a, zero) for a in solved(vec[0])]
+    for _ in range(REFINE):
+        rest = vec
+        for j in range(ITERS):
+            rest = pair_less(rest, pair_times(mat[j], c[j]))
+        c = [pair_add(a, (b, zero)) for a, b in zip(c, solved(rest[0]))]
     e = []
     for n in range(ITERS + 1):
-        total = jnp.ones_like(c[0]) if n == 0 else jnp.zeros_like(c[0])
+        total = (jnp.ones_like(zero), zero) if n == 0 else (zero, zero)
         if n < ITERS:
-            total = total - c[n]
+            total = pair_less(total, c[n])
         if n >= 1:
-            total = total + (1.0 if n == 1 else 0.5) * c[n - 1]
+            total = pair_add(total, c[0] if n == 1 else scaled(0.5, c[n - 1]))
         if n + 1 < ITERS:
-            total = total + 0.5 * c[n + 1]
-        e.append(total)
-    cs = [jnp.broadcast_to(a, (TILE, LANES)) for a in c]
-    es = [jnp.broadcast_to(a, (TILE, LANES)) for a in e]
+            total = pair_add(total, scaled(0.5, c[n + 1]))
+        e.append(total[0])
+    cs = [a[0] for a in c]
+    es = e
 
     def out_copy(which, to):
         return pltpu.make_async_remote_copy(
@@ -477,9 +607,10 @@
         return pl.pallas_call(
             functools.partial(kernel, axes),
             out_shape=(jax.ShapeDtypeStruct(volt_now.shape, f32),) * 2,
-            in_specs=[pl.BlockSpec(memory_space=pltpu.SMEM)] + [pl.BlockSpec(memory_space=pltpu.VMEM)] * 8,
+            in_specs=[pl.BlockSpec(memory_space=pltpu.SMEM)] + [pl.BlockSpec(memory_space=pl.ANY)] * 8,
             out_specs=(pl.BlockSpec(memory_space=pltpu.VMEM),) * 2,
-            scratch_shapes=[
+            scratch_shapes=[pltpu.VMEM(volt_now.shape, f32)] * 6 + [pltpu.VMEM(cell_ids.shape, jnp.int32)] * 2 + [
+                dma((8,)),
                 pltpu.VMEM((5, axes[2], group, cols // 2, LANES), f32),
                 pltpu.VMEM((5, layers, cols // 2, LANES), f32),
                 pltpu.VMEM((8, layers, tall, LANES), f32),
@@ -489,15 +620,15 @@
                 pltpu.VMEM((5, 2, tall, LANES), f32),
                 pltpu.VMEM((cols, LANES), f32),
                 pltpu.VMEM((2 * ITERS, TILE, LANES), f32),
-                pltpu.VMEM((4, max(axes), 2 * ITERS, LANES), f32),
+                pltpu.VMEM((2, axes[0] * axes[1], LANES), f32),
                 pltpu.VMEM((2, axes[2], group, cols // 2, LANES), f32),
                 pltpu.VMEM((2, axes[2], group, cols // 2, LANES), f32),
                 dma((5,)), dma((5,)), dma((5,)),
-                dma((5, 2)), dma((5, 2)), dma((5, 2)), dma((5, 2)),
+                dma((5, 2)), dma((5, 2)), dma((5, 2, 3)), dma((5, 2, 3)),
                 dma((3,)), dma((3,)), dma((2,)), dma((2,)), dma((2,)),
             ],
             compiler_params=pltpu.CompilerParams(
-                collective_id=0, has_side_effects=True, vmem_limit_bytes=48 << 20
+                collective_id=0, has_side_effects=True, vmem_limit_bytes=60 << 20
             ),
         )(current_table, volt_now, volt_prev, cap_term, edge_x, edge_y, via_below, cell_ids, placed)
 

time: 119 us -> 97.5 us (0.82)
  Pallas kernels: 108 us -> 94.3 us
  local copies, waits for them, and re-layouts: 9.56 us -> 2.42 us
    pallas_call x1, Pallas kernels: 108 us -> 94.3 us  [block(): pl.pallas_call(functools.partial(kernel, axes), out_shape=(jax.ShapeDtype...]
    unnamed x20 -> x4, local copies, waits for them, and re-layouts: 9.56 us -> 2.42 us
where the time goes in v2:
time: 97.5 us; the launch traced here: 97.4 us
  Pallas kernels  94.3 us (97%)
  local copies, waits for them, and re-layouts  2.42 us (2%)
    pallas_call x1, Pallas kernels, block(): pl.pallas_call(functools.partial(kernel, axes), out_shape=(jax.ShapeDtype...  94.3 us
    unnamed x4, local copies, waits for them, and re-layouts  2.42 us

profile of v2, /device:TPU:1, one launch (start us, length us, event | category | flops | bytes accessed | tf_op | source)
XLA Modules:
  0.0 97.4 jit_solution(10332930490742800369)
XLA Ops:
  0.6 94.3 %shard_map.104 = (f32[2,64,512]{2,1,0:T(8,128)}, f32[2,64,512]{2,1,0:T(8,128)}) custom-call(f32[64]{0:T(128)} %table.1, f32[2,64,512]{2,1,0:T(8,128)} %vn_h.1, f32[2,64,512]{2,1,0:T(8,128)} %vp_h.1, f32[2,64,512]{2,1,0:T(8,128)} %cap_h.1, f32[2,64,512]{2,1,0:T(8,128)} %ex_h.1, f32[2,64,512]{2,1,0:T(8,128)} %ey_h.1, f32[2,64,512]{2,1,0:T(8,128)} %vb_h.1, ...), custom_call_target="tpu_custom_call" | custom-call | tf_op jit(solution)/shard_map/pallas_call | solution.py:607
  94.9 0.0 copy-start
  95.0 1.7 %copy.13 = f32[2,64,512]{2,1,0:T(8,128)} copy(f32[2,64,512]{2,1,0:T(8,128)} %get-tuple-element.4) | data formatting | bytes 524288
  96.7 0.0 copy-done
  96.7 0.7 copy.14
Async XLA Ops:
  94.9 1.7 %copy-start = (f32[2,64,512]{2,1,0:T(8,128)S(1)}, f32[2,64,512]{2,1,0:T(8,128)}, u32[]{:S(2)}) copy-start(f32[2,64,512]{2,1,0:T(8,128)} %get-tuple-element.5) | copy-start | bytes 786436

commit v3 on v2

--- a/solution.py
+++ b/solution.py
@@ -14,7 +14,7 @@
 GHOST = 8
 TILE = 8
 LANES = 128
-AT_ONCE = 2
+AT_ONCE = 5
 REFINE = 3
 
 
@@ -60,7 +60,7 @@
 
 def kernel(
     axes, table, vn_h, vp_h, cap_h, ex_h, ey_h, vb_h, ids_h, placed_h, xo, ro,
-    vn, vp, cap, ex, ey, vb, ids, placed, in_s, pack, recv, coef, s_buf, u_buf, ysend, yrecv, cur, part, gath, packo, recvo,
+    vn, vp, cap, ex, ey, vb, ids, placed, in_s, pack, recv, coef, s_buf, u_buf, ysend, yrecv, cur, middle, part, gath, packo, recvo,
     t_ss, t_rs, l_s, x_ss, x_rs, y_ss, y_rs, r_ss, r_rs, o_ss, o_rs, lo_s,
 ):
     n_gx, n_gy, n_al = axes
@@ -292,6 +292,26 @@
         wait_array(which)
         unpack(which, c_of[which])
         start_edges(which, c_of[which])
+    wait_array(WI)
+
+    def sums_at_home(tile, c):
+        at = rows_at(tile + 1)
+        above = rows_at(jnp.maximum(tile, 1))
+        upper = tile // half_tiles
+        inner = jnp.logical_or(tile > 0, sub > 0)
+        for layer in range(layers):
+            held = recv[WI, layer, rows_at(tile % half_tiles)]
+            held = jnp.where(upper == 0, held, pltpu.roll(held, width, 1))
+            x, y = coef[EX, layer, at], coef[EY, layer, at]
+            held = held + (x + jnp.where(inner, before(x, coef[EX, layer, above]), 0.0)) + (y + pltpu.roll(y, 1, 1))
+            coef[WI, layer, at] = jnp.where(low, held, 0.0)
+        return c
+
+    lax.fori_loop(0, own_tiles, sums_at_home, 0)
+    start_edges(WI, c_of[WI])
+    wait_array(RHS)
+    unpack(RHS, u0)
+    start_edges(RHS, u0)
     finish_edges(EX, c_of[EX])
     finish_edges(EY, c_of[EY])
 
@@ -303,54 +323,53 @@
         return c
 
     lax.fori_loop(0, tiles, lefts, 0)
-    wait_array(WI)
-
-    def pivots(tile, c):
-        at = rows_at(tile + 1)
-        upper = tile // half_tiles
-        inverse = zero
-        for layer in range(layers):
-            held = recv[WI, layer, rows_at(tile % half_tiles)]
-            held = jnp.where(upper == 0, held, pltpu.roll(held, width, 1))
-            below = coef[VB, layer, at]
-            diag = held + coef[EX, layer, at] + coef[EXL, layer, at] + coef[EY, layer, at] + coef[EYL, layer, at] + below
-            if layer + 1 < layers:
-                diag = diag + coef[VB, layer + 1, at]
-            if layer:
-                diag = diag - below * below * inverse
-            inverse = jnp.where(low, 1.0 / diag, 0.0)
-            coef[WI, layer, at] = inverse
+    finish_edges(VB, c_of[VB])
+    finish_edges(WI, c_of[WI])
+
+    def pivots(turn_at, c):
+        each = [turn_at * AT_ONCE + step for step in range(AT_ONCE)]
+        mid = layers // 2
+        met = {}
+        for step, tile in enumerate(each):
+            at = rows_at(tile)
+            seam = jnp.logical_and(sub == 0, jnp.logical_or(tile == 1, tile == tiles - 1))
+            edge = jnp.logical_or(lane == 0, lane == width)
+            for rank in range(mid):
+                for layer, previous in ((rank, rank - 1), (layers - 1 - rank, layers - rank)):
+                    held = coef[WI, layer, at]
+                    below = coef[VB, layer, at]
+                    over = coef[VB, layer + 1, at] if layer + 1 < layers else zero
+                    diag = held + jnp.where(seam, coef[EXL, layer, at], 0.0)
+                    diag = diag + jnp.where(edge, coef[EYL, layer, at], 0.0)
+                    diag = diag + (below + over)
+                    if rank:
+                        link = below if previous < layer else over
+                        diag = diag - link * (link * met[step, previous])
+                    inverse = jnp.where(held > 0.0, 1.0 / diag, 0.0)
+                    met[step, layer] = inverse
+                    coef[WI, layer, at] = inverse
+                    coef[UP, layer, at] = below * inverse
+                    coef[DN, layer, at] = over * inverse
+            link = coef[VB, mid, at]
+            middle[at] = 1.0 / (1.0 - (link * met[step, mid - 1]) * (link * met[step, mid]))
         return c
 
-    lax.fori_loop(0, own_tiles, pivots, 0)
-    start_edges(WI, c_of[WI])
-    finish_edges(VB, c_of[VB])
-    wait_array(RHS)
-    unpack(RHS, u0)
-    start_edges(RHS, u0)
-    finish_edges(WI, c_of[WI])
-
-    def factors(tile, c):
-        at = rows_at(tile)
-        for layer in range(layers):
-            inverse = coef[WI, layer, at]
-            coef[UP, layer, at] = coef[VB, layer, at] * inverse
-            if layer + 1 < layers:
-                coef[DN, layer, at] = coef[VB, layer + 1, at] * inverse
-        return c
-
-    lax.fori_loop(0, tiles, factors, 0)
+    lax.fori_loop(0, tiles // AT_ONCE, pivots, 0)
     finish_edges(RHS, u0)
 
     def solve(us, at):
-        kept = []
-        d = None
-        for layer in range(layers):
-            term = us[layer] * coef[WI, layer, at]
-            d = term if layer == 0 else term + coef[UP, layer, at] * d
-            kept.append(d)
-        for layer in range(layers - 2, -1, -1):
-            kept[layer] = kept[layer] + coef[DN, layer, at] * kept[layer + 1]
+        mid = layers // 2
+        kept = [us[layer] * coef[WI, layer, at] for layer in range(layers)]
+        for rank in range(1, mid):
+            lo, hi = rank, layers - 1 - rank
+            kept[lo] = kept[lo] + coef[UP, lo, at] * kept[lo - 1]
+            kept[hi] = kept[hi] + coef[DN, hi, at] * kept[hi + 1]
+        kept[mid - 1] = middle[at] * (kept[mid - 1] + coef[DN, mid - 1, at] * kept[mid])
+        kept[mid] = kept[mid] + coef[UP, mid, at] * kept[mid - 1]
+        for rank in range(mid - 2, -1, -1):
+            lo, hi = rank, layers - 1 - rank
+            kept[lo] = kept[lo] + coef[DN, lo, at] * kept[lo + 1]
+            kept[hi] = kept[hi] + coef[UP, hi, at] * kept[hi - 1]
         return kept
 
     def is_own(tile):
@@ -372,17 +391,18 @@
     part[0] = lax.fori_loop(0, tiles // AT_ONCE, begin, zero)
 
     def apply(k, onward):
+        at_once = 5 if onward else 4
         twice = jnp.where(k == 0, 1.0, 2.0)
         once = jnp.where(k == 0, 0.0, 1.0)
         older = jnp.maximum(k - 1, 0)
 
         def one(turn_at, accs):
-            base = turn_at * AT_ONCE + (0 if onward else 1)
-            ats = [rows_at(base + step) for step in range(AT_ONCE)]
+            base = turn_at * at_once + (0 if onward else 1)
+            ats = [rows_at(base + step) for step in range(at_once)]
             above = rows_at(jnp.maximum(base - 1, 0))
-            under = rows_at(jnp.minimum(base + AT_ONCE, tiles - 1))
-            cross = [zero] * AT_ONCE
-            square = [zero] * AT_ONCE
+            under = rows_at(jnp.minimum(base + at_once, tiles - 1))
+            cross = [zero] * at_once
+            square = [zero] * at_once
             us = [[] for _ in ats]
             for layer in range(layers):
                 vs = [s_buf[k, layer, at] for at in [above] + ats + [under]]
@@ -403,13 +423,13 @@
                         s_buf[k + 1, layer, at] = ss[layer]
                         square[step] = square[step] + ss[layer] * us[step][layer]
             first_sum, second_sum = accs
-            for step in range(AT_ONCE):
+            for step in range(at_once):
                 own = is_own(base + step)
                 first_sum = first_sum + jnp.where(own, cross[step], 0.0)
                 second_sum = second_sum + jnp.where(own, square[step], 0.0)
             return first_sum, second_sum
 
-        cross, square = lax.fori_loop(0, (tiles if onward else own_tiles) // AT_ONCE, one, (zero, zero))
+        cross, square = lax.fori_loop(0, (tiles if onward else own_tiles) // at_once, one, (zero, zero))
         part[2 * k + 1] = cross
         if onward:
             part[2 * k + 2] = square
@@ -619,6 +639,7 @@
                 pltpu.VMEM((5, 2, tall, LANES), f32),
                 pltpu.VMEM((5, 2, tall, LANES), f32),
                 pltpu.VMEM((cols, LANES), f32),
+                pltpu.VMEM((tall, LANES), f32),
                 pltpu.VMEM((2 * ITERS, TILE, LANES), f32),
                 pltpu.VMEM((2, axes[0] * axes[1], LANES), f32),
                 pltpu.VMEM((2, axes[2], group, cols // 2, LANES), f32),

time: 97.5 us -> 88.8 us (0.911)
  Pallas kernels: 94.3 us -> 85.6 us
    pallas_call x1, Pallas kernels: 94.3 us -> 85.6 us  [block(): pl.pallas_call(functools.partial(kernel, axes), out_shape=(jax.ShapeDtype...]
where the time goes in v3:
time: 88.8 us; the launch traced here: 88.7 us
  Pallas kernels  85.6 us (96%)
  local copies, waits for them, and re-layouts  2.42 us (3%)
    pallas_call x1, Pallas kernels, block(): pl.pallas_call(functools.partial(kernel, axes), out_shape=(jax.ShapeDtype...  85.6 us
    unnamed x4, local copies, waits for them, and re-layouts  2.42 us

profile of v3, /device:TPU:1, one launch (start us, length us, event | category | flops | bytes accessed | tf_op | source)
XLA Modules:
  0.0 88.7 jit_solution(13522585568289621279)
XLA Ops:
  0.6 85.6 %shard_map.104 = (f32[2,64,512]{2,1,0:T(8,128)}, f32[2,64,512]{2,1,0:T(8,128)}) custom-call(f32[64]{0:T(128)} %table.1, f32[2,64,512]{2,1,0:T(8,128)} %vn_h.1, f32[2,64,512]{2,1,0:T(8,128)} %vp_h.1, f32[2,64,512]{2,1,0:T(8,128)} %cap_h.1, f32[2,64,512]{2,1,0:T(8,128)} %ex_h.1, f32[2,64,512]{2,1,0:T(8,128)} %ey_h.1, f32[2,64,512]{2,1,0:T(8,128)} %vb_h.1, ...), custom_call_target="tpu_custom_call" | custom-call | tf_op jit(solution)/shard_map/pallas_call | solution.py:627
  86.3 0.0 copy-start
  86.3 1.7 %copy.13 = f32[2,64,512]{2,1,0:T(8,128)} copy(f32[2,64,512]{2,1,0:T(8,128)} %get-tuple-element.4) | data formatting | bytes 524288
  88.0 0.0 copy-done
  88.0 0.7 copy.14
Async XLA Ops:
  86.3 1.7 %copy-start = (f32[2,64,512]{2,1,0:T(8,128)S(1)}, f32[2,64,512]{2,1,0:T(8,128)}, u32[]{:S(2)}) copy-start(f32[2,64,512]{2,1,0:T(8,128)} %get-tuple-element.5) | copy-start | bytes 786436

commit v4 on v3

--- a/solution.py
+++ b/solution.py
@@ -20,6 +20,15 @@
 
 def rows_at(tile):
     return pl.ds(pl.multiple_of(tile * TILE, TILE), TILE)
+
+
+def grouped(start, stop, at_once, one):
+    def turn(i, c):
+        for step in range(at_once):
+            one(start + i * at_once + step, c)
+        return c
+
+    lax.fori_loop(0, (stop - start) // at_once, turn, 0)
 
 
 def two_sum(a, b):
@@ -205,7 +214,7 @@
                 dest[layer, rows_at(tile + 1 + half_tiles)] = hi
             return c
 
-        lax.fori_loop(0, half_tiles, one, 0)
+        grouped(0, half_tiles, 2, one)
 
     def x_copies(which, dest):
         down = pltpu.make_async_remote_copy(
@@ -250,7 +259,7 @@
             ysend[which, 1, rows_at(tile)] = to_left
             return c
 
-        lax.fori_loop(1, own_tiles + 1, one, 0)
+        grouped(1, own_tiles + 1, 4, one)
         for copy in y_copies(which):
             copy.start()
 
@@ -277,7 +286,7 @@
                 dest[layer, rows_at(tile)] = jnp.where(outside, 0.0, jnp.where(low, v, edge))
             return c
 
-        lax.fori_loop(0, tiles, one, 0)
+        grouped(0, tiles, 5, one)
 
     def before(v, previous):
         return pltpu.roll(jnp.where(sub == TILE - 1, previous, v), 1, 0)
@@ -322,7 +331,7 @@
             coef[EYL, layer, rows_at(tile)] = pltpu.roll(coef[EY, layer, rows_at(tile)], 1, 1)
         return c
 
-    lax.fori_loop(0, tiles, lefts, 0)
+    grouped(0, tiles, 5, lefts)
     finish_edges(VB, c_of[VB])
     finish_edges(WI, c_of[WI])
 
@@ -391,7 +400,7 @@
     part[0] = lax.fori_loop(0, tiles // AT_ONCE, begin, zero)
 
     def apply(k, onward):
-        at_once = 5 if onward else 4
+        at_once = 10 if onward else 8
         twice = jnp.where(k == 0, 1.0, 2.0)
         once = jnp.where(k == 0, 0.0, 1.0)
         older = jnp.maximum(k - 1, 0)
@@ -582,7 +591,7 @@
                     packo[which, to, member, rows_at(tile)] = jnp.where(low, lo, pltpu.roll(hi, width, 1))
                     return carry
 
-                lax.fori_loop(0, half_tiles, one, 0)
+                grouped(0, half_tiles, half_tiles, one)
             if k:
                 out_copy(which, to).start()
             else:

time: 88.8 us -> 84.5 us (0.952)
  Pallas kernels: 85.6 us -> 81.3 us
    pallas_call x1, Pallas kernels: 85.6 us -> 81.3 us  [block(): pl.pallas_call(functools.partial(kernel, axes), out_shape=(jax.ShapeDtype...]
where the time goes in v4:
time: 84.5 us; the launch traced here: 84.4 us
  Pallas kernels  81.3 us (96%)
  local copies, waits for them, and re-layouts  2.42 us (3%)
    pallas_call x1, Pallas kernels, block(): pl.pallas_call(functools.partial(kernel, axes), out_shape=(jax.ShapeDtype...  81.3 us
    unnamed x4, local copies, waits for them, and re-layouts  2.42 us

profile of v4, /device:TPU:1, one launch (start us, length us, event | category | flops | bytes accessed | tf_op | source)
XLA Modules:
  0.0 84.4 jit_solution(14979186765946062902)
XLA Ops:
  0.6 81.3 %shard_map.104 = (f32[2,64,512]{2,1,0:T(8,128)}, f32[2,64,512]{2,1,0:T(8,128)}) custom-call(f32[64]{0:T(128)} %table.1, f32[2,64,512]{2,1,0:T(8,128)} %vn_h.1, f32[2,64,512]{2,1,0:T(8,128)} %vp_h.1, f32[2,64,512]{2,1,0:T(8,128)} %cap_h.1, f32[2,64,512]{2,1,0:T(8,128)} %ex_h.1, f32[2,64,512]{2,1,0:T(8,128)} %ey_h.1, f32[2,64,512]{2,1,0:T(8,128)} %vb_h.1, ...), custom_call_target="tpu_custom_call" | custom-call | tf_op jit(solution)/shard_map/pallas_call | solution.py:636
  81.9 0.0 copy-start
  81.9 1.7 %copy.13 = f32[2,64,512]{2,1,0:T(8,128)} copy(f32[2,64,512]{2,1,0:T(8,128)} %get-tuple-element.4) | data formatting | bytes 524288
  83.6 0.0 copy-done
  83.6 0.7 copy.14
Async XLA Ops:
  81.9 1.7 %copy-start = (f32[2,64,512]{2,1,0:T(8,128)S(1)}, f32[2,64,512]{2,1,0:T(8,128)}, u32[]{:S(2)}) copy-start(f32[2,64,512]{2,1,0:T(8,128)} %get-tuple-element.5) | copy-start | bytes 786436

commit v5 on v4

--- a/solution.py
+++ b/solution.py
@@ -214,7 +214,7 @@
                 dest[layer, rows_at(tile + 1 + half_tiles)] = hi
             return c
 
-        grouped(0, half_tiles, 2, one)
+        grouped(0, half_tiles, half_tiles, one)
 
     def x_copies(which, dest):
         down = pltpu.make_async_remote_copy(
@@ -316,7 +316,7 @@
             coef[WI, layer, at] = jnp.where(low, held, 0.0)
         return c
 
-    lax.fori_loop(0, own_tiles, sums_at_home, 0)
+    grouped(0, own_tiles, 4, sums_at_home)
     start_edges(WI, c_of[WI])
     wait_array(RHS)
     unpack(RHS, u0)
@@ -615,7 +615,7 @@
                     )
             return carry
 
-        lax.fori_loop(0, half_tiles, one, 0)
+        grouped(0, half_tiles, half_tiles, one)
 
     for which in range(5):
         many = recv.at[which, pl.ds(0, group * (n_al - 1))]

time: 84.5 us -> 84.3 us (level)
  no operation moved by 1% of the time
where the time goes in v5:
time: 84.3 us; the launch traced here: 84.1 us
  Pallas kernels  81.1 us (96%)
  local copies, waits for them, and re-layouts  2.42 us (3%)
    pallas_call x1, Pallas kernels, block(): pl.pallas_call(functools.partial(kernel, axes), out_shape=(jax.ShapeDtype...  81.1 us
    unnamed x4, local copies, waits for them, and re-layouts  2.42 us

profile of v5, /device:TPU:1, one launch (start us, length us, event | category | flops | bytes accessed | tf_op | source)
XLA Modules:
  0.0 84.1 jit_solution(5909876696653359420)
XLA Ops:
  0.6 81.1 %shard_map.104 = (f32[2,64,512]{2,1,0:T(8,128)}, f32[2,64,512]{2,1,0:T(8,128)}) custom-call(f32[64]{0:T(128)} %table.1, f32[2,64,512]{2,1,0:T(8,128)} %vn_h.1, f32[2,64,512]{2,1,0:T(8,128)} %vp_h.1, f32[2,64,512]{2,1,0:T(8,128)} %cap_h.1, f32[2,64,512]{2,1,0:T(8,128)} %ex_h.1, f32[2,64,512]{2,1,0:T(8,128)} %ey_h.1, f32[2,64,512]{2,1,0:T(8,128)} %vb_h.1, ...), custom_call_target="tpu_custom_call" | custom-call | tf_op jit(solution)/shard_map/pallas_call | solution.py:636
  81.7 0.0 copy-start
  81.7 1.7 %copy.13 = f32[2,64,512]{2,1,0:T(8,128)} copy(f32[2,64,512]{2,1,0:T(8,128)} %get-tuple-element.4) | data formatting | bytes 524288
  83.4 0.0 copy-done
  83.4 0.7 copy.14
Async XLA Ops:
  81.7 1.7 %copy-start = (f32[2,64,512]{2,1,0:T(8,128)S(1)}, f32[2,64,512]{2,1,0:T(8,128)}, u32[]{:S(2)}) copy-start(f32[2,64,512]{2,1,0:T(8,128)} %get-tuple-element.5) | copy-start | bytes 786436
